TPU v7x, 128 devices: a whole 4x4x4 slice. The times are simulated.
128 devices in a mesh: ctx: 8 (over x, core), exp: 16 (over y, z).
Axes of the slice: x: 4, y: 4, z: 4, core: 2. Of those that a mesh axis runs over, the one named last changes fastest.
Arguments:
- hidden_in: bfloat16 [8192, 2048], P(('ctx', 'exp')), may hold values from -6 to 6
- queries: bfloat16 [8192, 2048], P('ctx', 'exp'), may hold values from -72 to 72
- keys: bfloat16 [65536, 2048], P('ctx', 'exp'), may hold values from -6 to 6
- values: bfloat16 [65536, 2048], P('ctx', 'exp'), may hold values from -12 to 12
- block_choice: int32 [16, 8], replicated, may hold values from -1 to 15, as said below
- out_proj: bfloat16 [2048, 2048], P('exp'), may hold values from -0.125 to 0.125
- norm_gain: float32 [2048], replicated, may hold values from 0.1 to 1.9
- router: bfloat16 [2048, 16], replicated, may hold values from -0.25 to 0.25
- expert_ids: int32 [8192, 6], P(('ctx', 'exp')), may hold values from 0 to 15, all different within a row; in each aligned block of 64 rows (0 to 63, 64 to 127, ...) at most 36 rows name the same one
- w_gate: bfloat16 [16, 2048, 1408], P('exp'), may hold values from -0.125 to 0.125
- w_up: bfloat16 [16, 2048, 1408], P('exp'), may hold values from -0.125 to 0.125
- w_down: bfloat16 [16, 1408, 2048], P('exp'), may hold values from -0.15625 to 0.15625
Outputs:
- layer_out: bfloat16 [8192, 2048], P(('ctx', 'exp'))
Inputs may be any that keep to these rules, and one draw needn't show every extreme that they name: `block_choice`: row r lists the key blocks chosen by block r: its first entry is r, the others are distinct blocks before r; a row r < 7 holds -1 in its last 7 - r entries. `expert_ids`: each row names 6 different experts; the rows of one device name no expert more than 36 times.
All inputs are finite; a program needn't handle non-finite values.
Results may differ from a plain program's by a relative error of at most 0.02.
Values may be sent and summed in bfloat16 or wider, within the bound.
A program may use at most 192 MiB of HBM per device.

v0:
```python
import jax
import jax.numpy as jnp
from jax import lax
from jax.sharding import PartitionSpec as P

HD = 128
BLK = 4096


ROUTE_SCALE = 2.446
NORM_EPS = 1e-06


def attend_local(queries, key_all, value_all, block_choice, first_pos):
    rows_here, width_here = queries.shape
    heads_here = width_here // HD
    total_blocks = key_all.shape[0] // BLK
    key_blocks = key_all.reshape(total_blocks, BLK, heads_here, HD)
    value_blocks = value_all.reshape(total_blocks, BLK, heads_here, HD)
    own_block = first_pos // BLK
    picked = lax.dynamic_index_in_dim(block_choice, own_block, 0, keepdims=False)
    safe_picks = jnp.maximum(picked, 0)
    key_sel = key_blocks[safe_picks]
    value_sel = value_blocks[safe_picks]
    key_pos = safe_picks[:, None] * BLK + jnp.arange(BLK, dtype=jnp.int32)[None, :]
    listed = (picked >= 0)[None, None, :, None]
    foreign = (picked != own_block)[None, None, :, None]
    group_rows = min(128, rows_here)
    group_count = rows_here // group_rows
    query_groups = queries.reshape(group_count, group_rows, heads_here, HD)
    group_first = first_pos + jnp.arange(group_count, dtype=jnp.int32) * group_rows
    score_scale = HD ** (-0.5)

    def one_group(group_args):
        query_rows, group_start = group_args
        scores = (
            jnp.einsum("qhd,skhd->hqsk", query_rows, key_sel, preferred_element_type=jnp.float32)
            * score_scale
        )
        query_pos = group_start + jnp.arange(group_rows, dtype=jnp.int32)
        allowed = listed & (foreign | (key_pos[None, None, :, :] <= query_pos[None, :, None, None]))
        scores = jnp.where(allowed, scores, -jnp.inf)
        row_max = jnp.max(scores, axis=(2, 3), keepdims=True)
        exponentials = jnp.exp(scores - row_max)
        denominator = jnp.sum(exponentials, axis=(2, 3), keepdims=True)
        probabilities = (exponentials / denominator).astype(jnp.bfloat16)
        mixed = jnp.einsum(
            "hqsk,skhd->qhd", probabilities, value_sel, preferred_element_type=jnp.float32
        )
        return mixed.astype(jnp.bfloat16)

    attended = lax.map(one_group, (query_groups, group_first))
    return attended.reshape(rows_here, width_here)


def local(
    hidden_in,
    queries,
    keys,
    values,
    block_choice,
    out_proj,
    norm_gain,
    router,
    expert_ids,
    w_gate,
    w_up,
    w_down,
):
    key_all, value_all = (
        lax.all_gather(keys, "ctx", axis=0, tiled=True),
        lax.all_gather(values, "ctx", axis=0, tiled=True),
    )
    query_rows = queries.shape[0]
    first_pos = (
        key_all.shape[0] - query_rows * lax.axis_size("ctx") + lax.axis_index("ctx") * query_rows
    )
    attended = attend_local(queries, key_all, value_all, block_choice, first_pos)
    rows_here = hidden_in.shape[0]
    model_width = out_proj.shape[1]
    projected = lax.psum_scatter(
        jnp.dot(attended, out_proj, preferred_element_type=jnp.float32).astype(jnp.bfloat16),
        "exp",
        scatter_dimension=0,
        tiled=True,
    ).astype(jnp.float32)
    residual = (hidden_in.astype(jnp.float32) + projected).astype(jnp.bfloat16)
    residual_wide = residual.astype(jnp.float32)
    mean_square = jnp.mean(residual_wide * residual_wide, axis=1, keepdims=True)
    normed = (residual_wide * lax.rsqrt(mean_square + NORM_EPS) * norm_gain).astype(jnp.bfloat16)
    experts_all = router.shape[1]
    top_count = expert_ids.shape[1]
    capacity = min(rows_here, 3 * rows_here * top_count // (2 * experts_all))
    affinity = jax.nn.sigmoid(jnp.dot(normed, router, preferred_element_type=jnp.float32))
    onehot = expert_ids[:, :, None] == jnp.arange(experts_all, dtype=jnp.int32)[None, None, :]
    picked = jnp.sum(jnp.where(onehot, affinity[:, None, :], 0.0), axis=2)
    mix_weight = ROUTE_SCALE * picked / jnp.sum(picked, axis=1, keepdims=True)
    flat_hot = onehot.reshape(rows_here * top_count, experts_all).astype(jnp.int32)
    earlier_count = jnp.cumsum(flat_hot, axis=0) - flat_hot
    slot_index = jnp.sum(earlier_count * flat_hot, axis=1)
    position = expert_ids.reshape(-1) * capacity + slot_index
    token_of = jnp.arange(rows_here * top_count, dtype=jnp.int32) // top_count
    send_rows = (
        jnp.zeros((experts_all * capacity, model_width), jnp.bfloat16)
        .at[position]
        .set(normed[token_of])
    )
    send_rows = send_rows.reshape(experts_all, capacity, model_width)
    received = lax.all_to_all(send_rows, "exp", split_axis=0, concat_axis=0, tiled=True)
    item_count = received.shape[1]
    grouped = received.reshape(-1, w_gate.shape[0], item_count, model_width)
    gate_part = jnp.einsum("send,edf->senf", grouped, w_gate, preferred_element_type=jnp.float32)
    up_part = jnp.einsum("send,edf->senf", grouped, w_up, preferred_element_type=jnp.float32)
    hidden_units = (jax.nn.silu(gate_part) * up_part).astype(jnp.bfloat16)
    produced = jnp.einsum(
        "senf,efd->send", hidden_units, w_down, preferred_element_type=jnp.float32
    ).astype(jnp.bfloat16)
    returned = lax.all_to_all(
        produced.reshape(received.shape), "exp", split_axis=0, concat_axis=0, tiled=True
    )
    gathered = returned.reshape(experts_all * capacity, model_width)[position].reshape(
        rows_here, top_count, model_width
    )
    combined = jnp.sum(mix_weight[:, :, None] * gathered.astype(jnp.float32), axis=1)
    return (residual_wide + combined).astype(jnp.bfloat16)


def solution(mesh):
    placed = (
        P(("ctx", "exp"), None),
        P("ctx", "exp"),
        P("ctx", "exp"),
        P("ctx", "exp"),
        P(),
        P("exp", None),
        P(),
        P(),
        P(("ctx", "exp"), None),
        P("exp", None, None),
        P("exp", None, None),
        P("exp", None, None),
    )
    return jax.shard_map(
        local, mesh=mesh, in_specs=placed, out_specs=P(("ctx", "exp"), None), check_vma=False
    )
```

profile of v0, /device:TPU:0, one launch (start us, length us, event | category | flops | bytes accessed | tf_op | source)
XLA Modules:
  0.0 669.6 jit_solution(16485076540627109675)
XLA Ops:
  6.5 0.7 all-gather.3.cloned.1.call-update
  7.3 0.7 all-gather.5.cloned.1.call-update
  8.5 88.0 %all-gather.3.cloned.1.call-done = bf16[65536,128]{1,0:T(8,128)(2,1)} async-done(((bf16[8192,128]{1,0:T(8,128)(2,1)}), bf16[65536,128]{1,0:T(8,128)(2,1)}) %all-gather.3.cloned.1.call-update) | async-done | bytes 16777232 | tf_op jit(solution)/shard_map/all_gather | solution.py:71
  96.5 10.4 %gather_fusion = bf16[8,4096,128]{2,1,0:T(8,128)(2,1)} fusion(bf16[16,4096,128]{2,1,0:T(8,128)(2,1)} %bitcast.153, s32[1024]{0:T(1024)S(1)} %pad_clamp_fusion.2), kind=kCustom, calls=%fused_computation | custom fusion | bytes 16777248 | tf_op jit(solution)/shard_map/gather | solution.py:23
  106.9 76.9 %all-gather.5.cloned.1.call-done = bf16[65536,128]{1,0:T(8,128)(2,1)} async-done(((bf16[8192,128]{1,0:T(8,128)(2,1)}), bf16[65536,128]{1,0:T(8,128)(2,1)}) %all-gather.5.cloned.1.call-update) | async-done | bytes 16777232 | tf_op jit(solution)/shard_map/all_gather | solution.py:72
  183.8 10.4 %gather_fusion.1 = bf16[8,4096,128]{2,1,0:T(8,128)(2,1)} fusion(bf16[16,4096,128]{2,1,0:T(8,128)(2,1)} %bitcast.154, s32[1024]{0:T(1024)S(1)} %pad_clamp_fusion.2), kind=kCustom, calls=%fused_computation.1 | custom fusion | bytes 16777248 | tf_op jit(solution)/shard_map/gather | solution.py:24
  194.2 256.3 %while.11 = (s32[]{:T(128)}, bf16[8,128,1,128]{3,1,2,0:T(8,128)(2,1)S(1)}, pred[1,1,8,1]{2,3,1,0:T(4,128)(4,1)S(1)}, pred[1,1,8,1]{2,3,1,0:T(4,128)(4,1)S(1)}, s...) while((s32[]{:T(128)}, ...), condition=%wide.region_3.4_spmd.clone, body=%wide.region_0.3_spmd.clone.sunk | while | flops 2193670144 | bytes 67440808 | solution.py:52
  194.8 0.6 iota_add_fusion.4
  195.5 11.1 %fusion.70 = (f32[128]{0:T(128)S(1)}, f32[128,8,4096]{2,0,1:T(8,128)}) fusion(bf16[8,4096,1,128]{3,1,0,2:T(8,128)(2,1)} %get-tuple-element.185, bf16[8,128,1,128]{3,1,2,0:T(8,128)(2,1)} %get-tuple-element.184, s32[]{:T(128)} %get-tuple-element.169, s32[128]{0:T(128)S(1)} %iota_add_fusion.4, s32[8,4096]{1,0:T(8,128)S(1)} %iota_add_fusion.5, ...), kind=kOutput, calls=%fused_computation.86.clone.1 | convolution fusion | flops 1098907520 | bytes 25331216 | tf_op jit(solution)/shard_map/while/body/eval_jaxpr/qhd,skhd->hqsk/dot_general | solution.py:37
  206.6 8.2 %fusion.71 = f32[128]{0:T(128)S(1)} fusion(f32[128,8,4096]{2,0,1:T(8,128)} %get-tuple-element.157, f32[128]{0:T(128)S(1)} %get-tuple-element.158), kind=kLoop, calls=%fused_computation.9.clone.1 | loop fusion | flops 8388480 | bytes 16778240 | tf_op jit(solution)/shard_map/while/body/eval_jaxpr/reduce_sum | solution.py:45
  214.8 11.4 %fusion.72 = bf16[8,128,1,128]{3,1,2,0:T(8,128)(2,1)S(1)} fusion(bf16[8,128,1,128]{3,1,2,0:T(8,128)(2,1)S(1)} %get-tuple-element.170, s32[]{:T(128)} %get-tuple-element.169, bf16[8,4096,1,128]{3,1,0,2:T(8,128)(2,1)} %get-tuple-element.186, f32[128,8,4096]{2,0,1:T(8,128)} %get-tuple-element.157, f32[128]{0:T(128)S(1)} %fusion.71, ...), kind=kOutput, calls=%fused_computation.16.clone.1 | convolution fusion | flops 1086341120 | bytes 25199620 | tf_op jit(solution)/shard_map/while/body/eval_jaxpr/hqsk,skhd->qhd/dot_general | solution.py:47
  226.3 0.6 dynamic_slice.28
  226.9 0.6 iota_add_fusion.4
  227.6 11.1 %fusion.70 = (f32[128]{0:T(128)S(1)}, f32[128,8,4096]{2,0,1:T(8,128)}) fusion(bf16[8,4096,1,128]{3,1,0,2:T(8,128)(2,1)} %get-tuple-element.185, bf16[8,128,1,128]{3,1,2,0:T(8,128)(2,1)} %get-tuple-element.184, s32[]{:T(128)} %get-tuple-element.169, s32[128]{0:T(128)S(1)} %iota_add_fusion.4, s32[8,4096]{1,0:T(8,128)S(1)} %iota_add_fusion.5, ...), kind=kOutput, calls=%fused_computation.86.clone.1 | convolution fusion | flops 1098907520 | bytes 25331216 | tf_op jit(solution)/shard_map/while/body/eval_jaxpr/qhd,skhd->hqsk/dot_general | solution.py:37
  238.6 8.2 %fusion.71 = f32[128]{0:T(128)S(1)} fusion(f32[128,8,4096]{2,0,1:T(8,128)} %get-tuple-element.157, f32[128]{0:T(128)S(1)} %get-tuple-element.158), kind=kLoop, calls=%fused_computation.9.clone.1 | loop fusion | flops 8388480 | bytes 16778240 | tf_op jit(solution)/shard_map/while/body/eval_jaxpr/reduce_sum | solution.py:45
  246.9 11.4 %fusion.72 = bf16[8,128,1,128]{3,1,2,0:T(8,128)(2,1)S(1)} fusion(bf16[8,128,1,128]{3,1,2,0:T(8,128)(2,1)S(1)} %get-tuple-element.170, s32[]{:T(128)} %get-tuple-element.169, bf16[8,4096,1,128]{3,1,0,2:T(8,128)(2,1)} %get-tuple-element.186, f32[128,8,4096]{2,0,1:T(8,128)} %get-tuple-element.157, f32[128]{0:T(128)S(1)} %fusion.71, ...), kind=kOutput, calls=%fused_computation.16.clone.1 | convolution fusion | flops 1086341120 | bytes 25199620 | tf_op jit(solution)/shard_map/while/body/eval_jaxpr/hqsk,skhd->qhd/dot_general | solution.py:47
  258.3 0.6 dynamic_slice.28
  258.9 0.6 iota_add_fusion.4
  259.6 11.1 %fusion.70 = (f32[128]{0:T(128)S(1)}, f32[128,8,4096]{2,0,1:T(8,128)}) fusion(bf16[8,4096,1,128]{3,1,0,2:T(8,128)(2,1)} %get-tuple-element.185, bf16[8,128,1,128]{3,1,2,0:T(8,128)(2,1)} %get-tuple-element.184, s32[]{:T(128)} %get-tuple-element.169, s32[128]{0:T(128)S(1)} %iota_add_fusion.4, s32[8,4096]{1,0:T(8,128)S(1)} %iota_add_fusion.5, ...), kind=kOutput, calls=%fused_computation.86.clone.1 | convolution fusion | flops 1098907520 | bytes 25331216 | tf_op jit(solution)/shard_map/while/body/eval_jaxpr/qhd,skhd->hqsk/dot_general | solution.py:37
  270.7 8.2 %fusion.71 = f32[128]{0:T(128)S(1)} fusion(f32[128,8,4096]{2,0,1:T(8,128)} %get-tuple-element.157, f32[128]{0:T(128)S(1)} %get-tuple-element.158), kind=kLoop, calls=%fused_computation.9.clone.1 | loop fusion | flops 8388480 | bytes 16778240 | tf_op jit(solution)/shard_map/while/body/eval_jaxpr/reduce_sum | solution.py:45
  278.9 11.4 %fusion.72 = bf16[8,128,1,128]{3,1,2,0:T(8,128)(2,1)S(1)} fusion(bf16[8,128,1,128]{3,1,2,0:T(8,128)(2,1)S(1)} %get-tuple-element.170, s32[]{:T(128)} %get-tuple-element.169, bf16[8,4096,1,128]{3,1,0,2:T(8,128)(2,1)} %get-tuple-element.186, f32[128,8,4096]{2,0,1:T(8,128)} %get-tuple-element.157, f32[128]{0:T(128)S(1)} %fusion.71, ...), kind=kOutput, calls=%fused_computation.16.clone.1 | convolution fusion | flops 1086341120 | bytes 25199620 | tf_op jit(solution)/shard_map/while/body/eval_jaxpr/hqsk,skhd->qhd/dot_general | solution.py:47
  290.3 0.6 dynamic_slice.28
  290.9 0.6 iota_add_fusion.4
  291.6 11.1 %fusion.70 = (f32[128]{0:T(128)S(1)}, f32[128,8,4096]{2,0,1:T(8,128)}) fusion(bf16[8,4096,1,128]{3,1,0,2:T(8,128)(2,1)} %get-tuple-element.185, bf16[8,128,1,128]{3,1,2,0:T(8,128)(2,1)} %get-tuple-element.184, s32[]{:T(128)} %get-tuple-element.169, s32[128]{0:T(128)S(1)} %iota_add_fusion.4, s32[8,4096]{1,0:T(8,128)S(1)} %iota_add_fusion.5, ...), kind=kOutput, calls=%fused_computation.86.clone.1 | convolution fusion | flops 1098907520 | bytes 25331216 | tf_op jit(solution)/shard_map/while/body/eval_jaxpr/qhd,skhd->hqsk/dot_general | solution.py:37
  302.7 8.2 %fusion.71 = f32[128]{0:T(128)S(1)} fusion(f32[128,8,4096]{2,0,1:T(8,128)} %get-tuple-element.157, f32[128]{0:T(128)S(1)} %get-tuple-element.158), kind=kLoop, calls=%fused_computation.9.clone.1 | loop fusion | flops 8388480 | bytes 16778240 | tf_op jit(solution)/shard_map/while/body/eval_jaxpr/reduce_sum | solution.py:45
  310.9 11.4 %fusion.72 = bf16[8,128,1,128]{3,1,2,0:T(8,128)(2,1)S(1)} fusion(bf16[8,128,1,128]{3,1,2,0:T(8,128)(2,1)S(1)} %get-tuple-element.170, s32[]{:T(128)} %get-tuple-element.169, bf16[8,4096,1,128]{3,1,0,2:T(8,128)(2,1)} %get-tuple-element.186, f32[128,8,4096]{2,0,1:T(8,128)} %get-tuple-element.157, f32[128]{0:T(128)S(1)} %fusion.71, ...), kind=kOutput, calls=%fused_computation.16.clone.1 | convolution fusion | flops 1086341120 | bytes 25199620 | tf_op jit(solution)/shard_map/while/body/eval_jaxpr/hqsk,skhd->qhd/dot_general | solution.py:47
  322.4 0.6 dynamic_slice.28
  323.0 0.6 iota_add_fusion.4
  323.7 11.1 %fusion.70 = (f32[128]{0:T(128)S(1)}, f32[128,8,4096]{2,0,1:T(8,128)}) fusion(bf16[8,4096,1,128]{3,1,0,2:T(8,128)(2,1)} %get-tuple-element.185, bf16[8,128,1,128]{3,1,2,0:T(8,128)(2,1)} %get-tuple-element.184, s32[]{:T(128)} %get-tuple-element.169, s32[128]{0:T(128)S(1)} %iota_add_fusion.4, s32[8,4096]{1,0:T(8,128)S(1)} %iota_add_fusion.5, ...), kind=kOutput, calls=%fused_computation.86.clone.1 | convolution fusion | flops 1098907520 | bytes 25331216 | tf_op jit(solution)/shard_map/while/body/eval_jaxpr/qhd,skhd->hqsk/dot_general | solution.py:37
  334.7 8.2 %fusion.71 = f32[128]{0:T(128)S(1)} fusion(f32[128,8,4096]{2,0,1:T(8,128)} %get-tuple-element.157, f32[128]{0:T(128)S(1)} %get-tuple-element.158), kind=kLoop, calls=%fused_computation.9.clone.1 | loop fusion | flops 8388480 | bytes 16778240 | tf_op jit(solution)/shard_map/while/body/eval_jaxpr/reduce_sum | solution.py:45
  343.0 11.4 %fusion.72 = bf16[8,128,1,128]{3,1,2,0:T(8,128)(2,1)S(1)} fusion(bf16[8,128,1,128]{3,1,2,0:T(8,128)(2,1)S(1)} %get-tuple-element.170, s32[]{:T(128)} %get-tuple-element.169, bf16[8,4096,1,128]{3,1,0,2:T(8,128)(2,1)} %get-tuple-element.186, f32[128,8,4096]{2,0,1:T(8,128)} %get-tuple-element.157, f32[128]{0:T(128)S(1)} %fusion.71, ...), kind=kOutput, calls=%fused_computation.16.clone.1 | convolution fusion | flops 1086341120 | bytes 25199620 | tf_op jit(solution)/shard_map/while/body/eval_jaxpr/hqsk,skhd->qhd/dot_general | solution.py:47
  354.4 0.6 dynamic_slice.28
  355.0 0.6 iota_add_fusion.4
  355.7 11.1 %fusion.70 = (f32[128]{0:T(128)S(1)}, f32[128,8,4096]{2,0,1:T(8,128)}) fusion(bf16[8,4096,1,128]{3,1,0,2:T(8,128)(2,1)} %get-tuple-element.185, bf16[8,128,1,128]{3,1,2,0:T(8,128)(2,1)} %get-tuple-element.184, s32[]{:T(128)} %get-tuple-element.169, s32[128]{0:T(128)S(1)} %iota_add_fusion.4, s32[8,4096]{1,0:T(8,128)S(1)} %iota_add_fusion.5, ...), kind=kOutput, calls=%fused_computation.86.clone.1 | convolution fusion | flops 1098907520 | bytes 25331216 | tf_op jit(solution)/shard_map/while/body/eval_jaxpr/qhd,skhd->hqsk/dot_general | solution.py:37
  366.8 8.2 %fusion.71 = f32[128]{0:T(128)S(1)} fusion(f32[128,8,4096]{2,0,1:T(8,128)} %get-tuple-element.157, f32[128]{0:T(128)S(1)} %get-tuple-element.158), kind=kLoop, calls=%fused_computation.9.clone.1 | loop fusion | flops 8388480 | bytes 16778240 | tf_op jit(solution)/shard_map/while/body/eval_jaxpr/reduce_sum | solution.py:45
  375.0 11.4 %fusion.72 = bf16[8,128,1,128]{3,1,2,0:T(8,128)(2,1)S(1)} fusion(bf16[8,128,1,128]{3,1,2,0:T(8,128)(2,1)S(1)} %get-tuple-element.170, s32[]{:T(128)} %get-tuple-element.169, bf16[8,4096,1,128]{3,1,0,2:T(8,128)(2,1)} %get-tuple-element.186, f32[128,8,4096]{2,0,1:T(8,128)} %get-tuple-element.157, f32[128]{0:T(128)S(1)} %fusion.71, ...), kind=kOutput, calls=%fused_computation.16.clone.1 | convolution fusion | flops 1086341120 | bytes 25199620 | tf_op jit(solution)/shard_map/while/body/eval_jaxpr/hqsk,skhd->qhd/dot_general | solution.py:47
  386.4 0.6 dynamic_slice.28
  387.0 0.6 iota_add_fusion.4
  387.7 11.1 %fusion.70 = (f32[128]{0:T(128)S(1)}, f32[128,8,4096]{2,0,1:T(8,128)}) fusion(bf16[8,4096,1,128]{3,1,0,2:T(8,128)(2,1)} %get-tuple-element.185, bf16[8,128,1,128]{3,1,2,0:T(8,128)(2,1)} %get-tuple-element.184, s32[]{:T(128)} %get-tuple-element.169, s32[128]{0:T(128)S(1)} %iota_add_fusion.4, s32[8,4096]{1,0:T(8,128)S(1)} %iota_add_fusion.5, ...), kind=kOutput, calls=%fused_computation.86.clone.1 | convolution fusion | flops 1098907520 | bytes 25331216 | tf_op jit(solution)/shard_map/while/body/eval_jaxpr/qhd,skhd->hqsk/dot_general | solution.py:37
  398.8 8.2 %fusion.71 = f32[128]{0:T(128)S(1)} fusion(f32[128,8,4096]{2,0,1:T(8,128)} %get-tuple-element.157, f32[128]{0:T(128)S(1)} %get-tuple-element.158), kind=kLoop, calls=%fused_computation.9.clone.1 | loop fusion | flops 8388480 | bytes 16778240 | tf_op jit(solution)/shard_map/while/body/eval_jaxpr/reduce_sum | solution.py:45
  407.0 11.4 %fusion.72 = bf16[8,128,1,128]{3,1,2,0:T(8,128)(2,1)S(1)} fusion(bf16[8,128,1,128]{3,1,2,0:T(8,128)(2,1)S(1)} %get-tuple-element.170, s32[]{:T(128)} %get-tuple-element.169, bf16[8,4096,1,128]{3,1,0,2:T(8,128)(2,1)} %get-tuple-element.186, f32[128,8,4096]{2,0,1:T(8,128)} %get-tuple-element.157, f32[128]{0:T(128)S(1)} %fusion.71, ...), kind=kOutput, calls=%fused_computation.16.clone.1 | convolution fusion | flops 1086341120 | bytes 25199620 | tf_op jit(solution)/shard_map/while/body/eval_jaxpr/hqsk,skhd->qhd/dot_general | solution.py:47
  419.1 0.6 iota_add_fusion.4
  419.8 11.1 %fusion.70 = (f32[128]{0:T(128)S(1)}, f32[128,8,4096]{2,0,1:T(8,128)}) fusion(bf16[8,4096,1,128]{3,1,0,2:T(8,128)(2,1)} %get-tuple-element.185, bf16[8,128,1,128]{3,1,2,0:T(8,128)(2,1)} %get-tuple-element.184, s32[]{:T(128)} %get-tuple-element.169, s32[128]{0:T(128)S(1)} %iota_add_fusion.4, s32[8,4096]{1,0:T(8,128)S(1)} %iota_add_fusion.5, ...), kind=kOutput, calls=%fused_computation.86.clone.1 | convolution fusion | flops 1098907520 | bytes 25331216 | tf_op jit(solution)/shard_map/while/body/eval_jaxpr/qhd,skhd->hqsk/dot_general | solution.py:37
  430.9 8.2 %fusion.71 = f32[128]{0:T(128)S(1)} fusion(f32[128,8,4096]{2,0,1:T(8,128)} %get-tuple-element.157, f32[128]{0:T(128)S(1)} %get-tuple-element.158), kind=kLoop, calls=%fused_computation.9.clone.1 | loop fusion | flops 8388480 | bytes 16778240 | tf_op jit(solution)/shard_map/while/body/eval_jaxpr/reduce_sum | solution.py:45
  439.1 11.4 %fusion.72 = bf16[8,128,1,128]{3,1,2,0:T(8,128)(2,1)S(1)} fusion(bf16[8,128,1,128]{3,1,2,0:T(8,128)(2,1)S(1)} %get-tuple-element.170, s32[]{:T(128)} %get-tuple-element.169, bf16[8,4096,1,128]{3,1,0,2:T(8,128)(2,1)} %get-tuple-element.186, f32[128,8,4096]{2,0,1:T(8,128)} %get-tuple-element.157, f32[128]{0:T(128)S(1)} %fusion.71, ...), kind=kOutput, calls=%fused_computation.16.clone.1 | convolution fusion | flops 1086341120 | bytes 25199620 | tf_op jit(solution)/shard_map/while/body/eval_jaxpr/hqsk,skhd->qhd/dot_general | solution.py:47
  450.5 3.2 convolution_convert_fusion
  454.1 0.9 reduce-window.6
  455.8 76.6 %reduce-scatter.2.cloned.1.call-done = bf16[64,2048]{1,0:T(8,128)(2,1)} async-done(((bf16[1024,2048]{1,0:T(8,128)(2,1)}), bf16[64,2048]{1,0:T(8,128)(2,1)}) %reduce-scatter.2.cloned.1.call-update) | async-done | bytes 262160 | tf_op jit(solution)/shard_map/reduce_scatter | solution.py:81
  532.5 1.1 fusion.47
  533.6 1.1 fusion.49
  534.7 0.7 copy-done.4
  535.4 9.5 %scatter_custom_fusion = bf16[576,2048]{1,0:T(8,128)(2,1)} fusion(s32[384]{0:T(512)S(1)} %fusion.55, bf16[64,2048]{1,0:T(8,128)(2,1)S(1)} %fusion.49, s32[1024]{0:T(1024)S(1)} %pad_clamp_fusion.1, bf16[]{:T(256)} %constant.36.clone.1), kind=kCustom, calls=%fused_computation.39 | custom fusion | bytes 2359298 | tf_op jit(solution)/shard_map/scatter | solution.py:106
  544.9 2.6 reshape.258
  547.5 37.1 %all_to_all.10 = bf16[16,36,2048]{2,1,0:T(8,128)(2,1)S(1)} all-to-all(bf16[16,36,2048]{2,1,0:T(8,128)(2,1)S(1)} %reshape.258), channel_id=1, replica_groups=mesh['ctx'=8,'exp'=16] {'exp'}, dimensions={0} | all-to-all | bytes 4718592 | tf_op jit(solution)/shard_map/all_to_all | solution.py:109
  584.6 1.5 copy-done.1
  586.2 8.7 %fusion.23 = f32[16,36,1408]{2,1,0:T(8,128)} fusion(bf16[16,36,2048]{2,1,0:T(8,128)(2,1)S(1)} %all_to_all.10, bf16[1,2048,1408]{2,1,0:T(8,128)(2,1)} %param.24), kind=kOutput, calls=%fused_computation.24 | convolution fusion | flops 3321888768 | bytes 11370496 | tf_op jit(solution)/shard_map/send,edf->senf/dot_general | solution.py:113
  594.8 16.1 %fusion.33 = bf16[16,36,2048]{2,1,0:T(8,128)(2,1)} fusion(bf16[1,1408,2048]{2,1,0:T(8,128)(2,1)} %param.25, f32[16,36,1408]{2,1,0:T(8,128)} %fusion.23, bf16[16,36,2048]{2,1,0:T(8,128)(2,1)} %copy-done.1, bf16[1,2048,1408]{2,1,0:T(8,128)(2,1)} %param.23), kind=kOutput, calls=%fused_computation.37 | convolution fusion | flops 6649823232 | bytes 19496960 | tf_op jit(solution)/shard_map/senf,efd->send/dot_general | solution.py:115
  611.0 4.6 all-to-all-start.1
  615.9 32.8 %all-to-all-done.1 = bf16[16,36,2048]{2,1,0:T(8,128)(2,1)} async-done(((bf16[16,36,2048]{2,1,0:T(8,128)(2,1)}), bf16[16,36,2048]{2,1,0:T(8,128)(2,1)}, u32[]{:S(2)}, u32[]{:S(2)}) %all-to-all-start.1) | async-done | bytes 2359328 | tf_op jit(solution)/shard_map/all_to_all | solution.py:118
  648.8 2.7 reshape.263
  651.4 3.1 gather_fusion.2
  654.6 3.9 reshape.264
  658.5 3.7 multiply_reduce_fusion
  662.3 0.8 fusion.50
  (56 shorter events, 3.9 us)
Async XLA Ops:
  6.5 444.0 %copy-start = (bf16[128,2048]{1,0:T(8,128)(2,1)S(1)}, bf16[128,2048]{1,0:T(8,128)(2,1)}, u32[]{:S(2)}) copy-start(bf16[128,2048]{1,0:T(8,128)(2,1)} %param.19) | copy-start | bytes 1572868
  6.5 1.5 copy-start.8
  6.5 90.0 %all-gather.3.cloned.1.call-start = ((), (), s32[]{:S(2)}) async-start(), calls=%async_computation.3 | async-start | bytes 18874368 | tf_op jit(solution)/shard_map/all_gather | solution.py:71
  7.3 176.5 %all-gather.5.cloned.1.call-start = ((), (), s32[]{:S(2)}) async-start(), calls=%async_computation.4 | async-start | bytes 18874368 | tf_op jit(solution)/shard_map/all_gather | solution.py:72
  8.0 524.5 %reduce-scatter.2.cloned.1.call-start = ((), (), s32[]{:S(2)}) async-start(), calls=%async_computation.5 | async-start | bytes 4456448 | tf_op jit(solution)/shard_map/reduce_scatter | solution.py:81
  450.5 3.2 copy-start.7
  453.7 78.8 %copy-start.2 = (bf16[64,2048]{1,0:T(8,128)(2,1)S(1)}, bf16[64,2048]{1,0:T(8,128)(2,1)}, u32[]{:S(2)}) copy-start(bf16[64,2048]{1,0:T(8,128)(2,1)} %param.14) | copy-start | bytes 786436
  453.7 79.9 %copy-start.9 = (f32[2048]{0:T(1024)S(1)}, f32[2048]{0:T(1024)}, u32[]{:S(2)}) copy-start(f32[2048]{0:T(1024)} %param.20) | copy-start | bytes 24580
  534.7 0.7 copy-start.4
  584.6 1.5 copy-start.1
  611.0 4.6 copy-start.5
  611.0 4.6 copy-start.6
  611.0 37.8 %all-to-all-start.1 = ((bf16[16,36,2048]{2,1,0:T(8,128)(2,1)}), bf16[16,36,2048]{2,1,0:T(8,128)(2,1)}, u32[]{:S(2)}, u32[]{:S(2)}) async-start(bf16[16,36,2048]{2,1,0:T(8,128)(2,1)} %fusion.33), calls=%async_computation.2 | async-start | bytes 5242880 | tf_op jit(solution)/shard_map/all_to_all | solution.py:118
  654.6 7.7 %copy-start.3 = (bf16[64,2048]{1,0:T(8,128)(2,1)S(1)}, bf16[64,2048]{1,0:T(8,128)(2,1)}, u32[]{:S(2)}) copy-start(bf16[64,2048]{1,0:T(8,128)(2,1)} %reduce-scatter.2.cloned.1.call-done) | copy-start | bytes 786436
Sparse Core Ops, SparseCore 0:
  9.1 87.3 all-gather.2
  98.2 85.5 all-gather.4
  453.8 78.5 reduce-scatter.1
where the time goes:
time: 671 us; the launch traced here: 670 us
  waiting for transfers between devices  276 us (41%)
  matrix products  208 us (31%)
  other arithmetic  79.7 us (12%)
  local copies, waits for them, and re-layouts  50.7 us (8%)
  blocking collectives  37.1 us (6%)
  between operations  13.3 us (2%)
    dot_general x8, matrix products, one_group(): jnp.einsum('hqsk,skhd->qhd', probabilities, value_sel, preferred_element_...  91.3 us
    dot_general x8, matrix products, one_group(): jnp.einsum('qhd,skhd->hqsk', query_rows, key_sel, preferred_element_type=...  88.6 us
    all_gather x1, waiting for transfers between devices, local(): lax.all_gather(keys, 'ctx', axis=0, tiled=True)  88 us
    all_gather x1, waiting for transfers between devices, local(): lax.all_gather(values, 'ctx', axis=0, tiled=True)  76.9 us
    reduce_scatter x1, waiting for transfers between devices, local(): lax.psum_scatter(jnp.dot(attended, out_proj, preferred_element_type=jnp.f...  76.6 us
    reduce_sum x8, other arithmetic, one_group(): denominator = jnp.sum(exponentials, axis=(2, 3), keepdims=True)  65.7 us
    all_to_all x1, blocking collectives, local(): lax.all_to_all(send_rows, 'exp', split_axis=0, concat_axis=0, tiled=True)  37.1 us
    all_to_all x1, waiting for transfers between devices, local(): lax.all_to_all(produced.reshape(received.shape), 'exp', split_axis=0, con...  32.8 us
  transfers between devices with their start and end apart: 4, of which 4 were waited for; matrix products, arithmetic and copies ran while one was open for 2% of the time, Pallas kernels for 0%

commit v1 on v0

v1 whole, which is shorter than its diff:
```python
import functools

import jax
import jax.numpy as jnp
from jax import lax
from jax.experimental import pallas as pl
from jax.experimental.pallas import tpu as pltpu
from jax.sharding import PartitionSpec as P

HD = 128
BLK = 4096
ROUTE_SCALE = 2.446
NORM_EPS = 1e-06
LOG2E = 1.4426950408889634
LOW = -1e30
JUMP = 100.0
MESH = pl.DeviceIdType.MESH
MIB = 2**20

CHUNK = 1024
TQ = 512
SUB = 128
TKS = 1024
CHIPS = 4
SLOTS = 4
CAP = 36
TOK = 64
EXPERTS = 16
GROUP = EXPERTS * TOK


def nt(a, b):
    return lax.dot_general(a, b, (((1,), (1,)), ((), ())), preferred_element_type=jnp.float32)


def mm(a, b):
    return jnp.dot(a, b, preferred_element_type=jnp.float32)


def attention_kernel(
    choice, q_ref, k_own, k_oth, v_own, v_oth, o_ref, lse_ref,
    k_all, v_all, acc, m_s, l_s, r_s, mx_s, fresh, sems,
):
    scale = HD**-0.5 * LOG2E
    ctx = lax.axis_index("ctx")
    core = lax.rem(ctx, 2)
    other = ctx + 1 - 2 * core
    copies = []
    for slot in range(SLOTS):
        src_k, src_v = (k_own, v_own) if slot < 2 else (k_oth, v_oth)
        src = pl.ds((slot % 2) * BLK, BLK)
        dst = pl.ds(slot * BLK, BLK)
        copies.append(
            (
                pltpu.make_async_copy(src_k.at[src], k_all.at[dst], sems.at[0, slot]),
                pltpu.make_async_copy(src_v.at[src], v_all.at[dst], sems.at[1, slot]),
            )
        )
    for pair in copies:
        for copy in pair:
            copy.start()
    for pair in copies:
        for copy in pair:
            copy.wait()
    ones = jnp.ones((BLK, HD), jnp.bfloat16)

    def careful(q0, slot, steps, reach):
        @pl.loop(0, steps)
        def _(step):
            at = pl.ds(pl.multiple_of(slot * BLK + step * TKS, TKS), TKS)
            keys = k_all[at, :]
            vals = v_all[at, :]
            for i in range(TQ // SUB):
                rows = pl.ds(i * SUB, SUB)
                q = q_ref[pl.ds(pl.multiple_of(q0 + i * SUB, SUB), SUB), :]
                s = nt(q, keys) * scale
                key_pos = step * TKS + lax.broadcasted_iota(jnp.int32, (SUB, TKS), 1)
                query_pos = reach + i * SUB + lax.broadcasted_iota(jnp.int32, (SUB, TKS), 0)
                s = jnp.where(key_pos <= query_pos, s, LOW)
                old = m_s[rows]
                new = jnp.maximum(old, jnp.max(s, axis=1, keepdims=True))
                fade = jnp.exp2(old - new)
                p = jnp.exp2(s - new[:, :1])
                m_s[rows] = new
                l_s[rows] = l_s[rows] * fade + jnp.sum(p, axis=1, keepdims=True)
                acc[rows] = acc[rows] * fade + mm(p.astype(jnp.bfloat16), vals)

    def quick(q0, slot):
        base = pl.multiple_of(slot * BLK, BLK)
        keys = k_all[pl.ds(base, BLK), :]
        vals = jnp.concatenate([v_all[pl.ds(base, BLK), :], ones], axis=1)

        @pl.when(fresh[0] == 1)
        def _():
            some = k_all[pl.ds(base, 256), :]
            s = nt(q_ref[pl.ds(q0, TQ), :], some) * scale
            m_s[...] = jnp.broadcast_to(jnp.max(s, axis=1, keepdims=True), m_s.shape)

        for i in range(TQ // SUB):
            rows = pl.ds(i * SUB, SUB)
            q = q_ref[pl.ds(pl.multiple_of(q0 + i * SUB, SUB), SUB), :]
            s = nt(q, keys)
            old = m_s[rows]
            mx_s[rows] = jnp.broadcast_to(jnp.max(s, axis=1, keepdims=True) * scale, old.shape)
            p = jnp.exp2(s * scale - old[:, :1])
            r_s[rows] = mm(p.astype(jnp.bfloat16), vals)
        jump = jnp.max(mx_s[...] - m_s[...])

        @pl.when(jump <= JUMP)
        def _():
            old = m_s[...]
            new = jnp.maximum(old, mx_s[...])
            fade = jnp.exp2(old - new)
            m_s[...] = new
            acc[...] = (acc[...] + r_s[:, :HD]) * fade
            l_s[...] = (l_s[...] + r_s[:, HD:]) * fade

        @pl.when(jnp.logical_not(jump <= JUMP))
        def _():
            careful(q0, slot, BLK // TKS, BLK)

    @pl.loop(0, CHIPS * CHUNK // TQ)
    def _(tile):
        q0 = pl.multiple_of(tile * TQ, TQ)
        chunk = tile // (CHUNK // TQ)
        row = 14 + chunk // 2
        in_block = lax.rem(2 * chunk + core, 4) * CHUNK + lax.rem(tile, CHUNK // TQ) * TQ
        acc[...] = jnp.zeros_like(acc)
        l_s[...] = jnp.zeros_like(l_s)
        m_s[...] = jnp.full_like(m_s, LOW)
        fresh[0] = 1

        @pl.loop(0, SLOTS)
        def _(slot):
            block = jnp.where(slot < 2, 2 * ctx + slot, 2 * other + slot - 2)
            hit = choice[row, 1] == block
            for j in range(2, 8):
                hit = jnp.logical_or(hit, choice[row, j] == block)
            own = block == row

            @pl.when(own)
            def _():
                careful(q0, slot, in_block // TKS + 1, in_block)
                fresh[0] = 0

            @pl.when(jnp.logical_and(hit, jnp.logical_not(own)))
            def _():
                quick(q0, slot)
                fresh[0] = 0

        total = l_s[...]
        some = total > 0.0
        total = jnp.where(some, total, 1.0)
        o_ref[pl.ds(q0, TQ), :] = (acc[...] / total).astype(jnp.bfloat16)
        lse = jnp.where(some, m_s[...] + jnp.log2(total), LOW)
        flat = jnp.transpose(lse)
        for i in range(TQ // HD):
            lse_ref[pl.ds(tile * (TQ // HD) + i, 1), :] = flat[:1, i * HD : (i + 1) * HD]


def attend(choice, q_all, k_own, k_oth, v_own, v_oth):
    rows = CHIPS * CHUNK
    anywhere = pl.BlockSpec(memory_space=pl.ANY)
    vmem = pl.BlockSpec(memory_space=pltpu.VMEM)
    return pl.pallas_call(
        attention_kernel,
        out_shape=[
            jax.ShapeDtypeStruct((rows, HD), jnp.bfloat16),
            jax.ShapeDtypeStruct((rows // HD, HD), jnp.float32),
        ],
        in_specs=[pl.BlockSpec(memory_space=pltpu.SMEM), vmem] + [anywhere] * 4,
        out_specs=[vmem, vmem],
        scratch_shapes=[
            pltpu.VMEM((SLOTS * BLK, HD), jnp.bfloat16),
            pltpu.VMEM((SLOTS * BLK, HD), jnp.bfloat16),
            pltpu.VMEM((TQ, HD), jnp.float32),
            pltpu.VMEM((TQ, HD), jnp.float32),
            pltpu.VMEM((TQ, HD), jnp.float32),
            pltpu.VMEM((TQ, 2 * HD), jnp.float32),
            pltpu.VMEM((TQ, HD), jnp.float32),
            pltpu.SMEM((1,), jnp.int32),
            pltpu.SemaphoreType.DMA((2, SLOTS)),
        ],
        compiler_params=pltpu.CompilerParams(vmem_limit_bytes=56 * MIB),
        cost_estimate=pl.CostEstimate(
            flops=2 * 2 * rows * 2 * BLK * 2 * HD, bytes_accessed=20 * MIB, transcendentals=0
        ),
        name="attention",
    )(choice, q_all, k_own, k_oth, v_own, v_oth)


def merge_kernel(o_ref, lse_ref, out_ref, o_in, lse_in, send, recv):
    ctx = lax.axis_index("ctx")
    exp = lax.axis_index("exp")
    chip = ctx // 2
    core = lax.rem(ctx, 2)
    barrier = pltpu.get_barrier_semaphore()
    for d in range(1, CHIPS):
        peer = 2 * lax.rem(chip + d, CHIPS) + core
        pl.semaphore_signal(barrier, inc=1, device_id=(peer, exp), device_id_type=MESH)
    pl.semaphore_wait(barrier, CHIPS - 1)
    copies = []
    for d in (2, 1, 3):
        to = lax.rem(chip + d, CHIPS)
        peer = (2 * to + core, exp)
        for kind, src, dst in ((0, o_ref, o_in), (1, lse_ref, lse_in)):
            copy = pltpu.make_async_remote_copy(
                src_ref=src.at[to],
                dst_ref=dst.at[d - 1],
                send_sem=send.at[kind, d - 1],
                recv_sem=recv.at[kind, d - 1],
                device_id=peer,
                device_id_type=MESH,
            )
            copy.start()
            copies.append(copy)
    for copy in copies:
        copy.wait()
    parts = [lse_ref[chip]] + [lse_in[d] for d in range(CHIPS - 1)]
    top = functools.reduce(jnp.maximum, parts)
    weights = [jnp.exp2(part - top) for part in parts]
    total = functools.reduce(jnp.add, weights)
    columns = [jnp.transpose(weight / total) for weight in weights]
    for g in range(CHUNK // HD):
        rows = pl.ds(g * HD, HD)
        mixed = columns[0][:, g : g + 1] * o_ref[chip, rows, :].astype(jnp.float32)
        for d in range(CHIPS - 1):
            mixed += columns[d + 1][:, g : g + 1] * o_in[d, rows, :].astype(jnp.float32)
        out_ref[rows, :] = mixed.astype(jnp.bfloat16)


def merge(o, lse):
    vmem = pl.BlockSpec(memory_space=pltpu.VMEM)
    return pl.pallas_call(
        merge_kernel,
        out_shape=jax.ShapeDtypeStruct((CHUNK, HD), jnp.bfloat16),
        in_specs=[vmem, vmem],
        out_specs=vmem,
        scratch_shapes=[
            pltpu.VMEM((CHIPS - 1, CHUNK, HD), jnp.bfloat16),
            pltpu.VMEM((CHIPS - 1, CHUNK // HD, HD), jnp.float32),
            pltpu.SemaphoreType.DMA((2, CHIPS - 1)),
            pltpu.SemaphoreType.DMA((2, CHIPS - 1)),
        ],
        compiler_params=pltpu.CompilerParams(
            collective_id=0, has_side_effects=True, vmem_limit_bytes=32 * MIB
        ),
        name="merge",
    )(o.reshape(CHIPS, CHUNK, HD), lse.reshape(CHIPS, CHUNK // HD, HD))


ROWS = EXPERTS * CAP
FULL = ROWS + TOK


def expert_kernel(
    att_hbm, hid_hbm, proj_hbm, gate_hbm, up_hbm, down_hbm, ids_ref, gain_ref, router_ref,
    y_ref, res_ref,
    att, hid, proj, gate, up, down, picked, wide, normed, inner, sems,
):
    me = lax.axis_index("exp")
    width = hid.shape[1]
    copies = [
        pltpu.make_async_copy(src, dst, sems.at[i])
        for i, (src, dst) in enumerate(
            ((att_hbm, att), (hid_hbm, hid), (proj_hbm, proj), (gate_hbm, gate), (up_hbm, up), (down_hbm, down))
        )
    ]
    for copy in copies:
        copy.start()
    ids = ids_ref[...]
    chosen = functools.reduce(jnp.logical_or, [ids[j : j + 1] == me for j in range(6)])
    chosen_f = jnp.where(chosen, 1.0, 0.0)
    t_from = lax.broadcasted_iota(jnp.int32, (GROUP, GROUP), 0)
    t_to = lax.broadcasted_iota(jnp.int32, (GROUP, GROUP), 1)
    before = jnp.where((t_from < t_to) & (t_from // TOK == t_to // TOK), 1.0, 0.0)
    rank = mm(
        jnp.broadcast_to(chosen_f, (8, GROUP)).astype(jnp.bfloat16), before.astype(jnp.bfloat16)
    )[:1]
    token = lax.broadcasted_iota(jnp.int32, (1, GROUP), 1)
    place = jnp.where(chosen, (token // TOK) * CAP + rank.astype(jnp.int32), -1)
    own_place = jnp.where(token // TOK == me, ROWS + lax.rem(token, TOK), -1)
    row = lax.broadcasted_iota(jnp.int32, (FULL, GROUP), 0)
    select = jnp.where((row == place) | (row == own_place), 1.0, 0.0).astype(jnp.bfloat16)
    expert = lax.broadcasted_iota(jnp.int32, (EXPERTS, GROUP), 0)
    member = functools.reduce(jnp.logical_or, [ids[j : j + 1] == expert for j in range(6)])
    member_rows = nt(select, jnp.where(member, 1.0, 0.0).astype(jnp.bfloat16))
    copies[0].wait()
    for h in range(0, EXPERTS, 2):
        pair = jnp.concatenate([att[h], att[h + 1]], axis=1)
        picked[:, h * HD : (h + 2) * HD] = mm(select, pair).astype(jnp.bfloat16)
    copies[1].wait()
    copies[2].wait()

    step = 2 * HD

    @pl.loop(0, width // step)
    def _(c):
        cols = pl.ds(pl.multiple_of(c * step, step), step)
        base = mm(select, hid[:, cols])
        wide[:, cols] = (base + mm(picked[...], proj[:, cols])).astype(jnp.bfloat16)

    res_ref[...] = wide[ROWS:, :]
    for i in range(0, ROWS, 64):
        part = wide[i : i + 64, :].astype(jnp.float32)
        square = jnp.mean(part * part, axis=1, keepdims=True)
        normed[i : i + 64, :] = (part * lax.rsqrt(square + NORM_EPS) * gain_ref[...]).astype(jnp.bfloat16)
    affinity = jax.nn.sigmoid(mm(normed[...], router_ref[...]))
    lane = lax.broadcasted_iota(jnp.int32, affinity.shape, 1)
    mine = jnp.sum(jnp.where(lane == me, affinity, 0.0), axis=1, keepdims=True)
    everyone = jnp.sum(member_rows[:ROWS] * affinity, axis=1, keepdims=True)
    used = everyone > 0.0
    mix = jnp.where(used, ROUTE_SCALE * mine / jnp.where(used, everyone, 1.0), 0.0)
    copies[3].wait()
    copies[4].wait()
    hidden_units = gate.shape[1]
    for start in range(0, hidden_units, step):
        cols = slice(start, min(start + step, hidden_units))
        g = mm(normed[...], gate[:, cols])
        u = mm(normed[...], up[:, cols])
        inner[:, cols] = (g / (1.0 + jnp.exp(-g)) * u).astype(jnp.bfloat16)
    copies[5].wait()

    @pl.loop(0, width // step)
    def _(c):
        cols = pl.ds(pl.multiple_of(c * step, step), step)
        y_ref[:, cols] = (mm(inner[...], down[:, cols]) * mix).astype(jnp.bfloat16)


def experts(att_all, hid_all, proj_all, w_gate, w_up, w_down, ids_all, gain, router):
    width = hid_all.shape[1]
    units = w_gate.shape[1]
    anywhere = pl.BlockSpec(memory_space=pl.ANY)
    vmem = pl.BlockSpec(memory_space=pltpu.VMEM)
    bf16 = jnp.bfloat16
    return pl.pallas_call(
        expert_kernel,
        out_shape=[
            jax.ShapeDtypeStruct((ROWS, width), bf16),
            jax.ShapeDtypeStruct((TOK, width), bf16),
        ],
        in_specs=[anywhere] * 6 + [vmem] * 3,
        out_specs=[vmem, vmem],
        scratch_shapes=[
            pltpu.VMEM((EXPERTS, GROUP, HD), bf16),
            pltpu.VMEM((GROUP, width), bf16),
            pltpu.VMEM((width, width), bf16),
            pltpu.VMEM((width, units), bf16),
            pltpu.VMEM((width, units), bf16),
            pltpu.VMEM((units, width), bf16),
            pltpu.VMEM((FULL, width), bf16),
            pltpu.VMEM((FULL, width), bf16),
            pltpu.VMEM((ROWS, width), bf16),
            pltpu.VMEM((ROWS, units), bf16),
            pltpu.SemaphoreType.DMA((6,)),
        ],
        compiler_params=pltpu.CompilerParams(vmem_limit_bytes=60 * MIB),
        cost_estimate=pl.CostEstimate(
            flops=20 * 10**9, bytes_accessed=40 * MIB, transcendentals=0
        ),
        name="experts",
    )(att_all, hid_all, proj_all, w_gate, w_up, w_down, ids_all, gain, router)


def local(
    hidden_in, queries, keys, values, block_choice, out_proj, norm_gain, router, expert_ids,
    w_gate, w_up, w_down,
):
    width = hidden_in.shape[1]
    same_core = [[0, 2, 4, 6], [1, 3, 5, 7]]
    swap = [(i, i ^ 1) for i in range(8)]
    k_oth = lax.ppermute(keys, "ctx", swap)
    v_oth = lax.ppermute(values, "ctx", swap)
    q_all = lax.all_gather(queries, "ctx", axis=0, tiled=True, axis_index_groups=same_core)
    proj_all = lax.all_gather(out_proj, "exp", axis=0, tiled=True)
    hid_all = lax.all_gather(hidden_in, "exp", axis=0, tiled=True)
    ids_group = lax.all_gather(expert_ids, "exp", axis=0, tiled=True)
    ids_all = jnp.pad(ids_group.T, ((0, 2), (0, 0)), constant_values=-1)

    o, lse = attend(block_choice, q_all, keys, k_oth, values, v_oth)
    att = merge(o, lse)
    att_all = lax.all_gather(att, "exp", axis=0)
    y, residual = experts(
        att_all, hid_all, proj_all, w_gate[0], w_up[0], w_down[0], ids_all,
        norm_gain.reshape(1, width), router,
    )
    returned = lax.all_to_all(
        y.reshape(EXPERTS, CAP, width), "exp", split_axis=0, concat_axis=0, tiled=True
    ).reshape(ROWS, width)
    hot = expert_ids[:, :, None] == jnp.arange(EXPERTS, dtype=jnp.int32)[None, None, :]
    hot = jnp.any(hot, axis=1)
    rank = jnp.cumsum(hot.astype(jnp.int32), axis=0) - 1
    place = jnp.where(hot, jnp.arange(EXPERTS, dtype=jnp.int32)[None, :] * CAP + rank, -1)
    slot = jnp.arange(ROWS, dtype=jnp.int32)
    gather = jnp.repeat(place, CAP, axis=1, total_repeat_length=ROWS) == slot[None, :]
    combined = mm(gather.astype(jnp.bfloat16), returned)
    return (residual.astype(jnp.float32) + combined).astype(jnp.bfloat16)


def solution(mesh):
    placed = (
        P(("ctx", "exp"), None),
        P("ctx", "exp"),
        P("ctx", "exp"),
        P("ctx", "exp"),
        P(),
        P("exp", None),
        P(),
        P(),
        P(("ctx", "exp"), None),
        P("exp", None, None),
        P("exp", None, None),
        P("exp", None, None),
    )
    return jax.shard_map(
        local, mesh=mesh, in_specs=placed, out_specs=P(("ctx", "exp"), None), check_vma=False
    )
```

time: 671 us -> 354 us (0.53)
  matrix products: 208 us -> 2.99 us
  Pallas kernels: 0 us -> 122 us
  waiting for transfers between devices: 276 us -> 161 us
  other arithmetic: 79.7 us -> 0.14 us
  local copies, waits for them, and re-layouts: 50.7 us -> 14.5 us
    dot_general x20 -> x1, matrix products: 208 us -> 2.99 us  [mm(): return jnp.dot(a, b, preferred_element_type=jnp.float32)]
    pallas_call x0 -> x3, Pallas kernels: none -> 122 us  [the longest x1 47.6 us: merge(): pl.pallas_call(merge_kernel, out_shape=jax.ShapeDtypeStruct((CHUNK, HD),...]
    reduce_scatter x1 -> x0, waiting for transfers between devices: 76.6 us -> none  [local(): lax.psum_scatter(jnp.dot(attended, out_proj, preferred_element_type=jnp.f...]
    reduce_sum x12 -> x0, other arithmetic: 70.7 us -> none  [the longest x8 65.7 us: one_group(): denominator = jnp.sum(exponentials, axis=(2, 3), keepdims=True)]
    all_gather x2 -> x4, waiting for transfers between devices: 165 us -> 124 us  [the longest x1 72.5 us: local(): proj_all = lax.all_gather(out_proj, 'exp', axis=0, tiled=True)]
    all_to_all x1 -> x0, blocking collectives: 37.1 us -> none  [local(): lax.all_to_all(send_rows, 'exp', split_axis=0, concat_axis=0, tiled=True)]
    all_gather x0 -> x1, blocking collectives: none -> 33 us  [local(): ids_group = lax.all_gather(expert_ids, 'exp', axis=0, tiled=True)]
    gather x3 -> x1, local copies, waits for them, and re-layouts: 24 us -> 1.62 us  [local(): jnp.repeat(place, CAP, axis=1, total_repeat_length=ROWS) == slot[None, :]]
  transfers between devices with their start and end apart: 4 -> 7, of which waited for: 4 -> 4; matrix products, arithmetic and copies ran while one was open for 2% -> 1% of each run, Pallas kernels for 0% -> 26%
where the time goes in v1:
time: 354 us; the launch traced here: 353 us
  waiting for transfers between devices  161 us (45%)
  Pallas kernels  122 us (34%)
  blocking collectives  33 us (9%)
  local copies, waits for them, and re-layouts  14.5 us (4%)
  between operations  13.2 us (4%)
  starting transfers between devices  6.12 us (2%)
    all_gather x1, waiting for transfers between devices, local(): proj_all = lax.all_gather(out_proj, 'exp', axis=0, tiled=True)  72.5 us
    pallas_call x1, Pallas kernels, merge(): pl.pallas_call(merge_kernel, out_shape=jax.ShapeDtypeStruct((CHUNK, HD),...  47.6 us
    pallas_call x1, Pallas kernels, attend(): pl.pallas_call(attention_kernel, out_shape=[jax.ShapeDtypeStruct((rows, H...  42.5 us
    all_to_all x1, waiting for transfers between devices, local(): lax.all_to_all(y.reshape(EXPERTS, CAP, width), 'exp', split_axis=0, conca...  35 us
    all_gather x1, blocking collectives, local(): ids_group = lax.all_gather(expert_ids, 'exp', axis=0, tiled=True)  33 us
    pallas_call x1, Pallas kernels, experts(): pl.pallas_call(expert_kernel, out_shape=[jax.ShapeDtypeStruct((ROWS, widt...  32 us
    all_gather x1, waiting for transfers between devices, local(): att_all = lax.all_gather(att, 'exp', axis=0)  26.2 us
    all_gather x1, waiting for transfers between devices, local(): lax.all_gather(queries, 'ctx', axis=0, tiled=True, axis_index_groups=same...  25.5 us
  transfers between devices with their start and end apart: 7, of which 4 were waited for; matrix products, arithmetic and copies ran while one was open for 1% of the time, Pallas kernels for 26%

profile of v1, /device:TPU:0, one launch (start us, length us, event | category | flops | bytes accessed | tf_op | source)
XLA Modules:
  0.0 353.3 jit_solution(8855126078142229585)
XLA Ops:
  6.5 0.0 all-gather.7.cloned.1.call-start
  6.5 0.7 all-gather.7.cloned.1.call-update
  7.3 0.0 all-gather.9.cloned.1.call-start
  7.3 0.7 all-gather.9.cloned.1.call-update
  8.0 0.0 all-gather.13.cloned.1.call-start
  8.1 0.1 collective-permute-start
  8.1 0.5 collective-permute-start.1
  8.6 1.3 copy.28.choice
  10.0 0.0 copy-start.3
  10.0 25.5 %all-gather.7.cloned.1.call-done.q_ref = bf16[4096,128]{1,0:T(8,128)(2,1)} async-done(((bf16[1024,128]{1,0:T(8,128)(2,1)}), bf16[4096,128]{1,0:T(8,128)(2,1)}) %all-gather.7.cloned.1.call-update) | async-done | bytes 1048592 | tf_op jit(solution)/shard_map/all_gather | solution.py:374
  35.5 0.0 collective-permute-done.k_oth
  35.5 0.0 copy-start.6
  35.5 0.0 collective-permute-done.1.v_oth
  35.5 1.3 copy-done.6
  36.8 42.5 %attention.1 = (bf16[4096,128]{1,0:T(8,128)(2,1)}, f32[32,128]{1,0:T(8,128)}) custom-call(s32[16,8]{1,0:T(8,128)} %copy.28.choice, bf16[4096,128]{1,0:T(8,128)(2,1)} %all-gather.7.cloned.1.call-done.q_ref, bf16[8192,128]{1,0:T(8,128)(2,1)} %k_own.1, bf16[8192,128]{1,0:T(8,128)(2,1)} %copy-done.6, bf16[8192,128]{1,0:T(8,128)(2,1)} %v_own.1, ...), custom_call_target="tpu_custom_call" | custom-call | flops 34359738368 | bytes 20971520 | tf_op jit(solution)/shard_map/attention/pallas_call | solution.py:165
  79.3 0.0 copy-start.4
  79.4 0.0 copy-start
  79.4 1.2 copy-done
  80.6 0.0 copy-start.1
  80.6 0.7 copy-done.1
  81.3 47.6 %merge.1 = bf16[1024,128]{1,0:T(8,128)(2,1)} custom-call(bf16[4,1024,128]{2,1,0:T(8,128)(2,1)S(1)} %bitcast.15, f32[4,8,128]{2,1,0:T(8,128)S(1)} %bitcast.16), custom_call_target="tpu_custom_call" | custom-call | tf_op jit(solution)/shard_map/merge/pallas_call | solution.py:234
  128.9 0.0 all-gather.13.cloned.1.call-update
  128.9 0.0 all-gather.11.cloned.1.call-start
  129.0 0.5 all-gather.11.cloned.1.call-update
  129.5 0.0 copy-done.3
  129.5 1.0 copy.30.router_ref
  130.6 0.0 copy-done.4
  130.6 33.0 %all-gather.1 = s32[16,64,6]{1,2,0:T(8,128)S(1)} all-gather(s32[1,64,6]{1,2,0:T(8,128)S(1)} %bitcast.18), channel_id=1, replica_groups=mesh['ctx'=8,'exp'=16] {'exp'}, dimensions={0}, use_global_device_ids=true | all-gather | bytes 26112 | tf_op jit(solution)/shard_map/all_gather | solution.py:377
  163.6 0.1 reshape.80
  163.7 0.6 pad.8.ids_ref
  164.3 0.0 all-gather.9.cloned.1.call-done.hid_hbm
  164.3 26.2 %all-gather.13.cloned.1.call-done = bf16[16384,128]{1,0:T(8,128)(2,1)} async-done(((bf16[1024,128]{1,0:T(8,128)(2,1)}), bf16[16384,128]{1,0:T(8,128)(2,1)}) %all-gather.13.cloned.1.call-update) | async-done | bytes 4194320 | tf_op jit(solution)/shard_map/all_gather | solution.py:382
  190.5 72.5 %all-gather.11.cloned.1.call-done.proj_hbm = bf16[2048,2048]{1,0:T(8,128)(2,1)} async-done(((bf16[128,2048]{1,0:T(8,128)(2,1)}), bf16[2048,2048]{1,0:T(8,128)(2,1)}) %all-gather.11.cloned.1.call-update) | async-done | bytes 8388624 | tf_op jit(solution)/shard_map/all_gather | solution.py:375
  263.0 32.0 %experts.1 = (bf16[576,2048]{1,0:T(8,128)(2,1)}, bf16[64,2048]{1,0:T(8,128)(2,1)}) custom-call(bf16[16,1024,128]{2,1,0:T(8,128)(2,1)} %bitcast.22, bf16[1024,2048]{1,0:T(8,128)(2,1)} %all-gather.9.cloned.1.call-done.hid_hbm, bf16[2048,2048]{1,0:T(8,128)(2,1)} %all-gather.11.cloned.1.call-done.proj_hbm, bf16[2048,1408]{1,0:T(8,128)(2,1)} %bitcast.19, ...), custom_call_target="tpu_custom_call" | custom-call | flops 20000000000 | bytes 41943040 | tf_op jit(solution)/shard_map/experts/pallas_call | solution.py:336
  295.0 4.1 %reshape.68 = bf16[16,36,2048]{2,1,0:T(8,128)(2,1)} reshape(bf16[576,2048]{1,0:T(8,128)(2,1)} %get-tuple-element.24) | data formatting | bytes 4718592 | tf_op jit(solution)/shard_map/reshape | solution.py:388
  299.2 0.0 copy-start.5
  299.2 5.4 %all-to-all-start = ((bf16[16,36,2048]{2,1,0:T(8,128)(2,1)}), bf16[16,36,2048]{2,1,0:T(8,128)(2,1)S(1)}, u32[]{:S(2)}, u32[]{:S(2)}) async-start(bf16[16,36,2048]{2,1,0:T(8,128)(2,1)} %reshape.68), calls=%async_computation | async-start | bytes 5242880 | tf_op jit(solution)/shard_map/all_to_all | solution.py:387
  304.6 0.1 copy.32
  304.7 0.1 copy.31
  304.8 0.1 reduce_window_sum.26
  304.9 0.1 copy.33
  305.0 0.0 copy-done.5
  305.0 1.6 gather_fusion
  306.6 0.0 copy-start.2
  306.6 35.0 %all-to-all-done = bf16[16,36,2048]{2,1,0:T(8,128)(2,1)S(1)} async-done(((bf16[16,36,2048]{2,1,0:T(8,128)(2,1)}), bf16[16,36,2048]{2,1,0:T(8,128)(2,1)S(1)}, u32[]{:S(2)}, u32[]{:S(2)}) %all-to-all-start) | async-done | bytes 2359328 | tf_op jit(solution)/shard_map/all_to_all | solution.py:387
  341.7 2.1 reshape.69
  343.8 0.0 copy-done.2
  343.8 3.0 fusion
  (6 shorter events, 0.1 us)
Async XLA Ops:
  6.5 28.9 %all-gather.7.cloned.1.call-start = ((), (), s32[]{:S(2)}) async-start(), calls=%async_computation.1 | async-start | bytes 1310720 | tf_op jit(solution)/shard_map/all_gather | solution.py:374
  7.3 157.0 %all-gather.9.cloned.1.call-start = ((), (), s32[]{:S(2)}) async-start(), calls=%async_computation.2 | async-start | bytes 4456448 | tf_op jit(solution)/shard_map/all_gather | solution.py:376
  8.0 182.5 %all-gather.13.cloned.1.call-start = ((), (), s32[]{:S(2)}) async-start(), calls=%async_computation.4 | async-start | bytes 4456448 | tf_op jit(solution)/shard_map/all_gather | solution.py:382
  8.1 27.4 %collective-permute-start = (bf16[8192,128]{1,0:T(8,128)(2,1)}, bf16[8192,128]{1,0:T(8,128)(2,1)S(1)}, u32[]{:S(2)}, u32[]{:S(2)}) collective-permute-start(bf16[8192,128]{1,0:T(8,128)(2,1)} %k_own.1), channel_id=1, source_target_pairs={{0,16},{16,0},{32,48},{48,32},{64,80},{80,64},{96,112},{112,96},{1... | collective-permute-start | bytes 6291464 | tf_op jit(solution)/shard_map/ppermute | solution.py:372
  8.1 27.3 %collective-permute-start.1 = (bf16[8192,128]{1,0:T(8,128)(2,1)}, bf16[8192,128]{1,0:T(8,128)(2,1)}, u32[]{:S(2)}, u32[]{:S(2)}) collective-permute-start(bf16[8192,128]{1,0:T(8,128)(2,1)} %v_own.1), channel_id=1, source_target_pairs={{0,16},{16,0},{32,48},{48,32},{64,80},{80,64},{96,112},{112,96},{1... | collective-permute-start | bytes 6291464 | tf_op jit(solution)/shard_map/ppermute | solution.py:373
  10.0 119.5 %copy-start.3 = (bf16[2048,16]{0,1:T(8,128)(2,1)S(1)}, bf16[2048,16]{0,1:T(8,128)(2,1)}, u32[]{:S(2)}) copy-start(bf16[2048,16]{0,1:T(8,128)(2,1)} %param.21) | copy-start | bytes 196612
  35.5 1.3 copy-start.6
  79.3 51.2 %copy-start.4 = (s32[64,6]{0,1:T(8,128)S(1)}, s32[64,6]{0,1:T(8,128)}, u32[]{:S(2)}) copy-start(s32[64,6]{0,1:T(8,128)} %param.22) | copy-start | bytes 4612
  79.4 1.2 copy-start
  80.6 0.7 copy-start.1
  128.9 134.1 %all-gather.11.cloned.1.call-start = ((), (), s32[]{:S(2)}) async-start(), calls=%async_computation.3 | async-start | bytes 8912896 | tf_op jit(solution)/shard_map/all_gather | solution.py:375
  299.2 5.8 %copy-start.5 = (s32[576]{0:T(1024)S(1)}, s32[576]{0:T(1024)}, u32[]{:S(2)}) copy-start(s32[576]{0:T(1024)} %constant.104) | copy-start | bytes 6916
  299.2 42.5 %all-to-all-start = ((bf16[16,36,2048]{2,1,0:T(8,128)(2,1)}), bf16[16,36,2048]{2,1,0:T(8,128)(2,1)S(1)}, u32[]{:S(2)}, u32[]{:S(2)}) async-start(bf16[16,36,2048]{2,1,0:T(8,128)(2,1)} %reshape.68), calls=%async_computation | async-start | bytes 5242880 | tf_op jit(solution)/shard_map/all_to_all | solution.py:387
  306.6 37.2 %copy-start.2 = (bf16[64,2048]{1,0:T(8,128)(2,1)S(1)}, bf16[64,2048]{1,0:T(8,128)(2,1)}, u32[]{:S(2)}) copy-start(bf16[64,2048]{1,0:T(8,128)(2,1)} %get-tuple-element.23) | copy-start | bytes 786436
Sparse Core Ops, SparseCore 0:
  9.0 26.3 all-gather.6
  37.6 51.9 all-gather.8
  129.1 61.4 all-gather.12
  192.5 70.4 all-gather.10

commit v2 on v1

v2 whole, which is shorter than its diff:
```python
import functools

import jax
import jax.numpy as jnp
from jax import lax
from jax.experimental import pallas as pl
from jax.experimental.pallas import tpu as pltpu
from jax.sharding import PartitionSpec as P

HD = 128
BLK = 4096
ROUTE_SCALE = 2.446
NORM_EPS = 1e-06
LOG2E = 1.4426950408889634
LOW = -1e30
JUMP = 100.0
MESH = pl.DeviceIdType.MESH
MIB = 2**20

CHUNK = 1024
TQ = 512
SUB = 128
TKS = 1024
CHIPS = 4
SLOTS = 4
CAP = 36
TOK = 64
EXPERTS = 16
GROUP = EXPERTS * TOK


def nt(a, b):
    return lax.dot_general(a, b, (((1,), (1,)), ((), ())), preferred_element_type=jnp.float32)


def mm(a, b):
    return jnp.dot(a, b, preferred_element_type=jnp.float32)


def attention_kernel(
    choice, q_ref, k_own, k_oth, v_own, v_oth, o_ref, lse_ref,
    k_all, v_all, acc, m_s, l_s, r_s, mx_s, fresh, sems,
):
    scale = HD**-0.5 * LOG2E
    ctx = lax.axis_index("ctx")
    core = lax.rem(ctx, 2)
    other = ctx + 1 - 2 * core
    copies = []
    for slot in range(SLOTS):
        src_k, src_v = (k_own, v_own) if slot < 2 else (k_oth, v_oth)
        src = pl.ds((slot % 2) * BLK, BLK)
        dst = pl.ds(slot * BLK, BLK)
        copies.append(
            (
                pltpu.make_async_copy(src_k.at[src], k_all.at[dst], sems.at[0, slot]),
                pltpu.make_async_copy(src_v.at[src], v_all.at[dst], sems.at[1, slot]),
            )
        )
    for pair in copies:
        for copy in pair:
            copy.start()
    for pair in copies:
        for copy in pair:
            copy.wait()
    ones = jnp.ones((BLK, HD), jnp.bfloat16)

    def careful(q0, slot, steps, reach):
        @pl.loop(0, steps)
        def _(step):
            at = pl.ds(pl.multiple_of(slot * BLK + step * TKS, TKS), TKS)
            keys = k_all[at, :]
            vals = v_all[at, :]
            for i in range(TQ // SUB):
                rows = pl.ds(i * SUB, SUB)
                q = q_ref[pl.ds(pl.multiple_of(q0 + i * SUB, SUB), SUB), :]
                s = nt(q, keys) * scale
                key_pos = step * TKS + lax.broadcasted_iota(jnp.int32, (SUB, TKS), 1)
                query_pos = reach + i * SUB + lax.broadcasted_iota(jnp.int32, (SUB, TKS), 0)
                s = jnp.where(key_pos <= query_pos, s, LOW)
                old = m_s[rows]
                new = jnp.maximum(old, jnp.max(s, axis=1, keepdims=True))
                fade = jnp.exp2(old - new)
                p = jnp.exp2(s - new[:, :1])
                m_s[rows] = new
                l_s[rows] = l_s[rows] * fade + jnp.sum(p, axis=1, keepdims=True)
                acc[rows] = acc[rows] * fade + mm(p.astype(jnp.bfloat16), vals)

    def quick(q0, slot):
        base = pl.multiple_of(slot * BLK, BLK)
        keys = k_all[pl.ds(base, BLK), :]
        vals = jnp.concatenate([v_all[pl.ds(base, BLK), :], ones], axis=1)

        @pl.when(fresh[0] == 1)
        def _():
            some = k_all[pl.ds(base, 256), :]
            s = nt(q_ref[pl.ds(q0, TQ), :], some) * scale
            m_s[...] = jnp.broadcast_to(jnp.max(s, axis=1, keepdims=True), m_s.shape)

        for i in range(TQ // SUB):
            rows = pl.ds(i * SUB, SUB)
            q = q_ref[pl.ds(pl.multiple_of(q0 + i * SUB, SUB), SUB), :]
            s = nt(q, keys)
            old = m_s[rows]
            mx_s[rows] = jnp.broadcast_to(jnp.max(s, axis=1, keepdims=True) * scale, old.shape)
            p = jnp.exp2(s * scale - old[:, :1])
            r_s[rows] = mm(p.astype(jnp.bfloat16), vals)
        jump = jnp.max(mx_s[...] - m_s[...])

        @pl.when(jump <= JUMP)
        def _():
            old = m_s[...]
            new = jnp.maximum(old, mx_s[...])
            fade = jnp.exp2(old - new)
            m_s[...] = new
            acc[...] = (acc[...] + r_s[:, :HD]) * fade
            l_s[...] = (l_s[...] + r_s[:, HD:]) * fade

        @pl.when(jnp.logical_not(jump <= JUMP))
        def _():
            careful(q0, slot, BLK // TKS, BLK)

    @pl.loop(0, CHIPS * CHUNK // TQ)
    def _(tile):
        q0 = pl.multiple_of(tile * TQ, TQ)
        chunk = tile // (CHUNK // TQ)
        row = 14 + chunk // 2
        in_block = lax.rem(2 * chunk + core, 4) * CHUNK + lax.rem(tile, CHUNK // TQ) * TQ
        acc[...] = jnp.zeros_like(acc)
        l_s[...] = jnp.zeros_like(l_s)
        m_s[...] = jnp.full_like(m_s, LOW)
        fresh[0] = 1

        @pl.loop(0, SLOTS)
        def _(slot):
            block = jnp.where(slot < 2, 2 * ctx + slot, 2 * other + slot - 2)
            hit = choice[row, 1] == block
            for j in range(2, 8):
                hit = jnp.logical_or(hit, choice[row, j] == block)
            own = block == row

            @pl.when(own)
            def _():
                careful(q0, slot, in_block // TKS + 1, in_block)
                fresh[0] = 0

            @pl.when(jnp.logical_and(hit, jnp.logical_not(own)))
            def _():
                quick(q0, slot)
                fresh[0] = 0

        total = l_s[...]
        some = total > 0.0
        total = jnp.where(some, total, 1.0)
        o_ref[pl.ds(q0, TQ), :] = (acc[...] / total).astype(jnp.bfloat16)
        lse = jnp.where(some, m_s[...] + jnp.log2(total), LOW)
        flat = jnp.transpose(lse)
        for i in range(TQ // HD):
            lse_ref[pl.ds(tile * (TQ // HD) + i, 1), :] = flat[:1, i * HD : (i + 1) * HD]


def attend(choice, q_all, k_own, k_oth, v_own, v_oth):
    rows = CHIPS * CHUNK
    anywhere = pl.BlockSpec(memory_space=pl.ANY)
    vmem = pl.BlockSpec(memory_space=pltpu.VMEM)
    return pl.pallas_call(
        attention_kernel,
        out_shape=[
            jax.ShapeDtypeStruct((rows, HD), jnp.bfloat16),
            jax.ShapeDtypeStruct((rows // HD, HD), jnp.float32),
        ],
        in_specs=[pl.BlockSpec(memory_space=pltpu.SMEM), vmem] + [anywhere] * 4,
        out_specs=[vmem, vmem],
        scratch_shapes=[
            pltpu.VMEM((SLOTS * BLK, HD), jnp.bfloat16),
            pltpu.VMEM((SLOTS * BLK, HD), jnp.bfloat16),
            pltpu.VMEM((TQ, HD), jnp.float32),
            pltpu.VMEM((TQ, HD), jnp.float32),
            pltpu.VMEM((TQ, HD), jnp.float32),
            pltpu.VMEM((TQ, 2 * HD), jnp.float32),
            pltpu.VMEM((TQ, HD), jnp.float32),
            pltpu.SMEM((1,), jnp.int32),
            pltpu.SemaphoreType.DMA((2, SLOTS)),
        ],
        compiler_params=pltpu.CompilerParams(vmem_limit_bytes=56 * MIB),
        cost_estimate=pl.CostEstimate(
            flops=2 * 2 * rows * 2 * BLK * 2 * HD, bytes_accessed=20 * MIB, transcendentals=0
        ),
        name="attention",
    )(choice, q_all, k_own, k_oth, v_own, v_oth)


def share_kernel(q_ref, k_ref, v_ref, ids_ref, q_all, k_oth, v_oth, ids_all, send, recv, near):
    ctx = lax.axis_index("ctx")
    me = lax.axis_index("exp")
    chip = ctx // 2
    core = lax.rem(ctx, 2)
    twin = (ctx + 1 - 2 * core, me)
    x_peers = [(2 * lax.rem(chip + d, CHIPS) + core, me) for d in range(1, CHIPS)]
    e_peers = [(ctx, lax.rem(me + d, EXPERTS)) for d in range(1, EXPERTS)]
    barrier = pltpu.get_barrier_semaphore()
    for peer in [twin] + x_peers + e_peers:
        pl.semaphore_signal(barrier, inc=1, device_id=peer, device_id_type=MESH)
    mine = [
        pltpu.make_async_copy(q_ref, q_all.at[chip], near.at[0]),
        pltpu.make_async_copy(ids_ref, ids_all.at[me], near.at[1]),
    ]
    for copy in mine:
        copy.start()
    pl.semaphore_wait(barrier, 1 + len(x_peers) + len(e_peers))
    copies = []

    def send_to(src, dst, peer):
        n = len(copies)
        copy = pltpu.make_async_remote_copy(
            src_ref=src, dst_ref=dst, send_sem=send.at[n], recv_sem=recv.at[n],
            device_id=peer, device_id_type=MESH,
        )
        copy.start()
        copies.append(copy)

    for d in (2, 1, 3):
        send_to(q_ref, q_all.at[chip], x_peers[d - 1])
    for part in range(2):
        at = pl.ds(part * BLK, BLK)
        send_to(k_ref.at[at], k_oth.at[at], twin)
        send_to(v_ref.at[at], v_oth.at[at], twin)
    for peer in e_peers:
        send_to(ids_ref, ids_all.at[me], peer)
    for copy in copies + mine:
        copy.wait()


def share(queries, keys, values, ids):
    anywhere = pl.BlockSpec(memory_space=pl.ANY)
    copies = CHIPS - 1 + 4 + EXPERTS - 1
    return pl.pallas_call(
        share_kernel,
        out_shape=[
            jax.ShapeDtypeStruct((CHIPS,) + queries.shape, queries.dtype),
            jax.ShapeDtypeStruct(keys.shape, keys.dtype),
            jax.ShapeDtypeStruct(values.shape, values.dtype),
            jax.ShapeDtypeStruct((EXPERTS,) + ids.shape, ids.dtype),
        ],
        in_specs=[anywhere] * 4,
        out_specs=[anywhere] * 4,
        scratch_shapes=[
            pltpu.SemaphoreType.DMA((copies,)),
            pltpu.SemaphoreType.DMA((copies,)),
            pltpu.SemaphoreType.DMA((2,)),
        ],
        compiler_params=pltpu.CompilerParams(collective_id=0, has_side_effects=True),
        name="share",
    )(queries, keys, values, ids)


SIDE = 4
PACK = SIDE * CAP
LINE = SIDE * TOK
ROWS = EXPERTS * CAP
HALF = 1024
STEP = 256


def post_kernel(
    o_ref, lse_ref, hid_ref, ids_ref, gain_ref, router_ref, proj_hbm, gate_hbm, up_hbm, down_hbm,
    out_ref,
    o_in, lse_in, att, heads, proj, gate, up, down, wide, nall, picked, inner, turned, y_out,
    y_in, z_out, z_in,
    near, x_send, x_recv, a_send, a_recv, g_send, g_recv, r_send, r_recv,
):
    ctx = lax.axis_index("ctx")
    me = lax.axis_index("exp")
    chip = ctx // 2
    core = lax.rem(ctx, 2)
    yy = me // SIDE
    zz = lax.rem(me, SIDE)
    width = hid_ref.shape[1]

    def along(axis, d):
        if axis == 0:
            return lax.rem(yy + d, SIDE) * SIDE + zz
        return yy * SIDE + lax.rem(zz + d, SIDE)

    loads = [
        pltpu.make_async_copy(src, dst, near.at[i])
        for i, (src, dst) in enumerate(
            ((proj_hbm, proj), (gate_hbm, gate), (up_hbm, up), (down_hbm, down))
        )
    ]
    for load in loads:
        load.start()
    barrier = pltpu.get_barrier_semaphore()
    for d in range(1, CHIPS):
        peer = (2 * lax.rem(chip + d, CHIPS) + core, me)
        pl.semaphore_signal(barrier, inc=1, device_id=peer, device_id_type=MESH)
    for d in range(1, EXPERTS):
        peer = (ctx, lax.rem(me + d, EXPERTS))
        pl.semaphore_signal(barrier, inc=1, device_id=peer, device_id_type=MESH)
    pl.semaphore_wait(barrier, CHIPS - 1 + EXPERTS - 1)

    def remote(src, dst, send, recv, peer):
        copy = pltpu.make_async_remote_copy(
            src_ref=src, dst_ref=dst, send_sem=send, recv_sem=recv,
            device_id=peer, device_id_type=MESH,
        )
        copy.start()
        return copy

    x_copies = []
    for d in (2, 1, 3):
        to = lax.rem(chip + d, CHIPS)
        peer = (2 * to + core, me)
        for kind, src, dst in ((0, o_ref, o_in), (1, lse_ref, lse_in)):
            x_copies.append(
                remote(src.at[to], dst.at[d - 1], x_send.at[kind, d - 1], x_recv.at[kind, d - 1], peer)
            )

    t_to = lax.broadcasted_iota(jnp.int32, (LINE, LINE), 0)
    t_from = lax.broadcasted_iota(jnp.int32, (LINE, LINE), 1)
    before = jnp.where((t_from < t_to) & (t_from // TOK == t_to // TOK), 1.0, 0.0).astype(jnp.bfloat16)
    base = (lax.broadcasted_iota(jnp.int32, (LINE, HD), 0) // TOK) * CAP
    slot = lax.broadcasted_iota(jnp.int32, (LINE, LINE), 1)

    def packing(ids, expert):
        chosen = functools.reduce(jnp.logical_or, [ids[:, j : j + 1] == expert for j in range(6)])
        chosen = jnp.broadcast_to(chosen, (LINE, HD))
        rank = mm(before, jnp.where(chosen, 1.0, 0.0).astype(jnp.bfloat16)).astype(jnp.int32)
        place = jnp.where(chosen, base + rank, -1)
        return jnp.where(slot == place[:, :1], 1.0, 0.0)

    lane = lax.broadcasted_iota(jnp.int32, (LINE, HD), 1)
    selects = []
    members = []
    for g in range(SIDE):
        ids = jnp.concatenate([ids_ref[g * SIDE + i] for i in range(SIDE)], axis=0)
        select = jnp.transpose(packing(ids, me))[:PACK].astype(jnp.bfloat16)
        member = functools.reduce(jnp.logical_or, [ids[:, j : j + 1] == lane for j in range(6)])
        selects.append(select)
        members.append(mm(select, jnp.where(member, 1.0, 0.0).astype(jnp.bfloat16)))

    for copy in x_copies:
        copy.wait()
    parts = [lse_ref[chip]] + [lse_in[d] for d in range(CHIPS - 1)]
    top = functools.reduce(jnp.maximum, parts)
    weights = [jnp.exp2(part - top) for part in parts]
    total = functools.reduce(jnp.add, weights)
    columns = [jnp.transpose(weight / total) for weight in weights]
    for g in range(CHUNK // HD):
        rows = pl.ds(g * HD, HD)
        mixed = columns[0][:, g : g + 1] * o_ref[chip, rows, :].astype(jnp.float32)
        for d in range(CHIPS - 1):
            mixed += columns[d + 1][:, g : g + 1] * o_in[d, rows, :].astype(jnp.float32)
        att[2 * g] = mixed[:TOK].astype(jnp.bfloat16)
        att[2 * g + 1] = mixed[TOK:].astype(jnp.bfloat16)
    a_copies = []
    for d in range(1, EXPERTS):
        to = lax.rem(me + d, EXPERTS)
        a_copies.append(
            remote(att.at[to], heads.at[me], a_send.at[d - 1], a_recv.at[d - 1], (ctx, to))
        )
    heads[me] = att[me]
    loads[0].wait()
    for copy in a_copies:
        copy.wait()
    joined = jnp.concatenate([heads[h] for h in range(EXPERTS)], axis=1)

    @pl.loop(0, width // STEP)
    def _(c):
        cols = pl.ds(pl.multiple_of(c * STEP, STEP), STEP)
        wide[:, cols] = hid_ref[:, cols].astype(jnp.float32) + mm(joined, proj[:, cols])

    residual = wide[...].astype(jnp.bfloat16).astype(jnp.float32)
    wide[...] = residual
    square = jnp.mean(residual * residual, axis=1, keepdims=True)
    normed = (residual * lax.rsqrt(square + NORM_EPS) * gain_ref[...]).astype(jnp.bfloat16)
    nall[0, me] = normed[:, :HALF]
    nall[1, me] = normed[:, HALF:]

    top_rows, low_rows = pl.ds(0, TOK // 2), pl.ds(TOK // 2, TOK // 2)
    g_copies = []

    def pass_on(half, owner, rows, axis, d, n):
        view = nall.at[half, owner] if rows is None else nall.at[half, owner, rows]
        copy = remote(view, view, g_send.at[half, n], g_recv.at[half, n], (ctx, along(axis, d)))
        g_copies.append(copy)
        return copy

    def owner_at(half, first, second):
        dy, dz = (second, first) if half == 0 else (first, second)
        return lax.rem(yy + dy, SIDE) * SIDE + lax.rem(zz + dz, SIDE)

    firsts = (1, 0)
    seconds = (0, 1)
    stage1 = {}
    stage2 = {}
    for half in range(2):
        for n, d in ((0, 1), (1, 3)):
            stage1[half, d] = pass_on(half, me, None, firsts[half], d, n)
        for n, d in ((4, 1), (5, 3)):
            stage2[half, 0, d] = pass_on(half, me, None, seconds[half], d, n)
    for half in range(2):
        stage1[half, 1].wait_recv()
        stage1[half, 10] = pass_on(half, owner_at(half, 3, 0), top_rows, firsts[half], 1, 2)
        stage1[half, 3].wait_recv()
        stage1[half, 30] = pass_on(half, owner_at(half, 1, 0), low_rows, firsts[half], 3, 3)
        for first, n in ((3, 8), (1, 12)):
            for d in (1, 3):
                stage2[half, first, d] = pass_on(
                    half, owner_at(half, first, 0), None, seconds[half], d, n + d // 2
                )
    for half in range(2):
        stage2[half, 0, 1].wait_recv()
        pass_on(half, owner_at(half, 0, 3), top_rows, seconds[half], 1, 6)
        stage2[half, 0, 3].wait_recv()
        pass_on(half, owner_at(half, 0, 1), low_rows, seconds[half], 3, 7)
    for half in range(2):
        stage1[half, 10].wait_recv()
        stage1[half, 30].wait_recv()
        for d in (1, 3):
            stage2[half, 2, d] = pass_on(
                half, owner_at(half, 2, 0), None, seconds[half], d, 16 + d // 2
            )
    for first, n in ((3, 10), (1, 14), (2, 18)):
        for half in range(2):
            stage2[half, first, 1].wait_recv()
            pass_on(half, owner_at(half, first, 3), top_rows, seconds[half], 1, n)
            stage2[half, first, 3].wait_recv()
            pass_on(half, owner_at(half, first, 1), low_rows, seconds[half], 3, n + 1)
    arrived = list(stage1.values()) + list(stage2.values())
    for copy in g_copies:
        if not any(copy is seen for seen in arrived):
            copy.wait_recv()
    for copy in g_copies:
        copy.wait_send()

    for g in range(SIDE):
        rows = pl.ds(g * PACK, PACK)
        for half in range(2):
            line = jnp.concatenate([nall[half, g * SIDE + i] for i in range(SIDE)], axis=0)
            picked[rows, half * HALF : (half + 1) * HALF] = mm(selects[g], line).astype(jnp.bfloat16)
    affinity = jax.nn.sigmoid(mm(picked[...], router_ref[...]))
    expert = lax.broadcasted_iota(jnp.int32, affinity.shape, 1)
    mine = jnp.sum(jnp.where(expert == me, affinity, 0.0), axis=1, keepdims=True)
    member = jnp.concatenate(members, axis=0)
    everyone = jnp.sum(member[:, :EXPERTS] * affinity, axis=1, keepdims=True)
    used = everyone > 0.0
    mix = jnp.where(used, ROUTE_SCALE * mine / jnp.where(used, everyone, 1.0), 0.0)
    loads[1].wait()
    loads[2].wait()
    units = gate.shape[1]
    for start in range(0, units, STEP):
        cols = slice(start, min(start + STEP, units))
        gated = mm(picked[...], gate[:, cols])
        raised = mm(picked[...], up[:, cols])
        inner[:, cols] = (gated / (1.0 + jnp.exp(-gated)) * raised).astype(jnp.bfloat16)
    to_row = lax.broadcasted_iota(jnp.int32, (ROWS, ROWS), 0)
    from_row = lax.broadcasted_iota(jnp.int32, (ROWS, ROWS), 1)
    owner = to_row // CAP
    source = (lax.rem(owner, SIDE) * SIDE + owner // SIDE) * CAP + lax.rem(to_row, CAP)
    turn = jnp.where(from_row == source, 1.0, 0.0).astype(jnp.bfloat16)
    turned[...] = mm(turn, inner[...]).astype(jnp.bfloat16)
    mix_high = mix.astype(jnp.bfloat16)
    mix_low = (mix - mix_high.astype(jnp.float32)).astype(jnp.bfloat16)
    mix_turned = mm(turn, jnp.broadcast_to(mix_high, (ROWS, HD))) + mm(
        turn, jnp.broadcast_to(mix_low, (ROWS, HD))
    )
    loads[3].wait()
    r_copies = {}
    for half in range(2):
        rows_in = inner if half == 0 else turned
        share_of = mix if half == 0 else mix_turned[:, :1]

        @pl.loop(0, HALF // STEP)
        def _(c):
            cols = pl.ds(pl.multiple_of(c * STEP, STEP), STEP)
            from_cols = pl.ds(pl.multiple_of(half * HALF + c * STEP, STEP), STEP)
            y = mm(rows_in[...], down[:, from_cols]) * share_of
            for g in range(SIDE):
                y_out[half, g, :, cols] = y[g * PACK : (g + 1) * PACK].astype(jnp.bfloat16)

        at = yy if half == 0 else zz
        for d in (2, 1, 3):
            r_copies[half, 0, d] = remote(
                y_out.at[half, lax.rem(at + d, SIDE)], y_in.at[half, d - 1],
                r_send.at[half, 0, d - 1], r_recv.at[half, 0, d - 1], (ctx, along(half, d)),
            )

    sums = []
    for half in range(2):
        at = yy if half == 0 else zz
        owners = [yy * SIDE + i if half == 0 else i * SIDE + zz for i in range(SIDE)]
        ids = jnp.concatenate([ids_ref[owner] for owner in owners], axis=0)
        summed = mm(
            packing(ids, me)[:, :PACK].astype(jnp.bfloat16), y_out[half, at]
        )
        for d in (1, 3, 2):
            expert_from = along(half, SIDE - d)
            spread = packing(ids, expert_from)[:, :PACK].astype(jnp.bfloat16)
            r_copies[half, 0, d].wait_recv()
            summed += mm(spread, y_in[half, d - 1])
        for i in range(SIDE):
            z_out[half, i] = summed[i * TOK : (i + 1) * TOK].astype(jnp.bfloat16)
        here = zz if half == 0 else yy
        for d in (2, 1, 3):
            r_copies[half, 1, d] = remote(
                z_out.at[half, lax.rem(here + d, SIDE)], z_in.at[half, d - 1],
                r_send.at[half, 1, d - 1], r_recv.at[half, 1, d - 1], (ctx, along(1 - half, d)),
            )
    for half in range(2):
        here = zz if half == 0 else yy
        cols = slice(half * HALF, (half + 1) * HALF)
        result = wide[:, cols] + z_out[half, here].astype(jnp.float32)
        for d in (1, 3, 2):
            r_copies[half, 1, d].wait_recv()
            result += z_in[half, d - 1].astype(jnp.float32)
        out_ref[:, cols] = result.astype(jnp.bfloat16)
    for copy in r_copies.values():
        copy.wait_send()


def post(o, lse, hidden_in, ids, gain, router, proj, w_gate, w_up, w_down):
    width = hidden_in.shape[1]
    units = w_gate.shape[1]
    anywhere = pl.BlockSpec(memory_space=pl.ANY)
    vmem = pl.BlockSpec(memory_space=pltpu.VMEM)
    bf16 = jnp.bfloat16
    dma = pltpu.SemaphoreType.DMA
    return pl.pallas_call(
        post_kernel,
        out_shape=jax.ShapeDtypeStruct((TOK, width), bf16),
        in_specs=[vmem] * 6 + [anywhere] * 4,
        out_specs=vmem,
        scratch_shapes=[
            pltpu.VMEM((CHIPS - 1, CHUNK, HD), bf16),
            pltpu.VMEM((CHIPS - 1, CHUNK // HD, HD), jnp.float32),
            pltpu.VMEM((EXPERTS, TOK, HD), bf16),
            pltpu.VMEM((EXPERTS, TOK, HD), bf16),
            pltpu.VMEM((width, width), bf16),
            pltpu.VMEM((width, units), bf16),
            pltpu.VMEM((width, units), bf16),
            pltpu.VMEM((units, width), bf16),
            pltpu.VMEM((TOK, width), jnp.float32),
            pltpu.VMEM((2, EXPERTS, TOK, HALF), bf16),
            pltpu.VMEM((ROWS, width), bf16),
            pltpu.VMEM((ROWS, units), bf16),
            pltpu.VMEM((ROWS, units), bf16),
            pltpu.VMEM((2, SIDE, PACK, HALF), bf16),
            pltpu.VMEM((2, SIDE - 1, PACK, HALF), bf16),
            pltpu.VMEM((2, SIDE, TOK, HALF), bf16),
            pltpu.VMEM((2, SIDE - 1, TOK, HALF), bf16),
            dma((4,)),
            dma((2, CHIPS - 1)),
            dma((2, CHIPS - 1)),
            dma((EXPERTS - 1,)),
            dma((EXPERTS - 1,)),
            dma((2, 20)),
            dma((2, 20)),
            dma((2, 2, SIDE - 1)),
            dma((2, 2, SIDE - 1)),
        ],
        compiler_params=pltpu.CompilerParams(
            collective_id=1, has_side_effects=True, vmem_limit_bytes=62 * MIB
        ),
        name="post",
    )(
        o.reshape(CHIPS, CHUNK, HD), lse.reshape(CHIPS, CHUNK // HD, HD), hidden_in, ids, gain,
        router, proj, w_gate, w_up, w_down,
    )


def local(
    hidden_in, queries, keys, values, block_choice, out_proj, norm_gain, router, expert_ids,
    w_gate, w_up, w_down,
):
    width = hidden_in.shape[1]
    proj_all = lax.all_gather(out_proj, "exp", axis=0, tiled=True)
    ids = jnp.pad(expert_ids, ((0, 0), (0, HD - expert_ids.shape[1])), constant_values=-1)
    q_all, k_oth, v_oth, ids_all = share(queries, keys, values, ids)
    o, lse = attend(
        block_choice, q_all.reshape(CHIPS * CHUNK, HD), keys, k_oth, values, v_oth
    )
    return post(
        o, lse, hidden_in, ids_all, norm_gain.reshape(1, width), router, proj_all,
        w_gate[0], w_up[0], w_down[0],
    )


def solution(mesh):
    placed = (
        P(("ctx", "exp"), None),
        P("ctx", "exp"),
        P("ctx", "exp"),
        P("ctx", "exp"),
        P(),
        P("exp", None),
        P(),
        P(),
        P(("ctx", "exp"), None),
        P("exp", None, None),
        P("exp", None, None),
        P("exp", None, None),
    )
    return jax.shard_map(
        local, mesh=mesh, in_specs=placed, out_specs=P(("ctx", "exp"), None), check_vma=False
    )
```

time: 354 us -> 203 us (0.57)
  the two profiles are of different devices: /device:TPU:0 before, /device:TPU:1 now
where the time goes in v2:
time: 203 us; the launch traced here: 202 us
  Pallas kernels  165 us (81%)
  waiting for transfers between devices  18 us (9%)
  between operations  13.4 us (7%)
  local copies, waits for them, and re-layouts  6.27 us (3%)
    pallas_call x1, Pallas kernels, post(): pl.pallas_call(post_kernel, out_shape=jax.ShapeDtypeStruct((TOK, width),...  110 us
    pallas_call x1, Pallas kernels, attend(): pl.pallas_call(attention_kernel, out_shape=[jax.ShapeDtypeStruct((rows, H...  31.8 us
    pallas_call x1, Pallas kernels, share(): pl.pallas_call(share_kernel, out_shape=[jax.ShapeDtypeStruct((CHIPS,) + q...  22.7 us
    all_gather x1, waiting for transfers between devices, local(): proj_all = lax.all_gather(out_proj, 'exp', axis=0, tiled=True)  17.3 us
    unnamed x4, local copies, waits for them, and re-layouts  5.65 us
  transfers between devices with their start and end apart: 1, of which 1 were waited for; matrix products, arithmetic and copies ran while one was open for 2% of the time, Pallas kernels for 27%

profile of v2, /device:TPU:1, one launch (start us, length us, event | category | flops | bytes accessed | tf_op | source)
XLA Modules:
  0.0 202.3 jit_solution(4907385861461025982)
XLA Ops:
  6.5 0.0 all-gather.2.cloned.1.call-start
  6.5 0.7 all-gather.2.cloned.1.call-update
  7.3 0.8 copy.13
  8.0 1.3 copy.14.choice
  9.4 1.9 copy.15.router_ref
  11.2 0.6 pad.4.ids_ref
  11.9 22.7 %share.1 = (bf16[4,1024,128]{2,1,0:T(8,128)(2,1)}, bf16[8192,128]{1,0:T(8,128)(2,1)}, bf16[8192,128]{1,0:T(8,128)(2,1)}, s32[16,64,128]{2,1,0:T(8,128)}) custom-call(bf16[1024,128]{1,0:T(8,128)(2,1)} %q_ref.1, bf16[8192,128]{1,0:T(8,128)(2,1)} %k_own.1, bf16[8192,128]{1,0:T(8,128)(2,1)} %v_own.1, s32[64,128]{1,0:T(8,128)} %pad.4.ids_ref), custom_call_target="tpu_custom_call" | custom-call | tf_op jit(solution)/shard_map/share/pallas_call | solution.py:236
  34.5 31.8 %attention.1 = (bf16[4096,128]{1,0:T(8,128)(2,1)}, f32[32,128]{1,0:T(8,128)}) custom-call(s32[16,8]{1,0:T(8,128)} %copy.14.choice, bf16[4096,128]{1,0:T(8,128)(2,1)} %bitcast.13, bf16[8192,128]{1,0:T(8,128)(2,1)} %k_own.1, bf16[8192,128]{1,0:T(8,128)(2,1)} %get-tuple-element.12.k_oth, bf16[8192,128]{1,0:T(8,128)(2,1)} %v_own.1, ...), custom_call_target="tpu_custom_call" | custom-call | flops 34359738368 | bytes 20971520 | tf_op jit(solution)/shard_map/attention/pallas_call | solution.py:165
  66.4 17.3 %all-gather.2.cloned.1.call-done.proj_hbm = bf16[2048,2048]{1,0:T(8,128)(2,1)} async-done(((bf16[128,2048]{1,0:T(8,128)(2,1)}), bf16[2048,2048]{1,0:T(8,128)(2,1)}) %all-gather.2.cloned.1.call-update) | async-done | bytes 8388624 | tf_op jit(solution)/shard_map/all_gather | solution.py:576
  83.6 110.2 %post.1 = bf16[64,2048]{1,0:T(8,128)(2,1)} custom-call(bf16[4,1024,128]{2,1,0:T(8,128)(2,1)} %bitcast.10, f32[4,8,128]{2,1,0:T(8,128)} %bitcast.11, bf16[64,2048]{1,0:T(8,128)(2,1)} %hid_ref.1, s32[16,64,128]{2,1,0:T(8,128)} %get-tuple-element.16.ids_ref, f32[1,2048]{1,0:T(1,128)} %bitcast.12, bf16[2048,16]{1,0:T(8,128)(2,1)} %copy.15.router_ref, ...), custom_call_target="tpu_custom_call" | custom-call | tf_op jit(solution)/shard_map/post/pallas_call | solution.py:528
  193.8 1.7 copy.17
Async XLA Ops:
  6.5 77.1 %all-gather.2.cloned.1.call-start = ((), (), s32[]{:S(2)}) async-start(), calls=%async_computation | async-start | bytes 8912896 | tf_op jit(solution)/shard_map/all_gather | solution.py:576
Sparse Core Ops, SparseCore 0:
  9.5 74.0 all-gather.1

commit v3 on v2

v3 whole, which is shorter than its diff:
```python
import functools

import jax
import jax.numpy as jnp
from jax import lax
from jax.experimental import pallas as pl
from jax.experimental.pallas import tpu as pltpu
from jax.sharding import PartitionSpec as P

HD = 128
BLK = 4096
ROUTE_SCALE = 2.446
NORM_EPS = 1e-06
LOG2E = 1.4426950408889634
LOW = -1e30
JUMP = 100.0
MESH = pl.DeviceIdType.MESH
MIB = 2**20

CHUNK = 1024
TQ = 512
SUB = 128
TKS = 1024
CHIPS = 4
SLOTS = 4
CAP = 36
TOK = 64
EXPERTS = 16
GROUP = EXPERTS * TOK


def nt(a, b):
    return lax.dot_general(a, b, (((1,), (1,)), ((), ())), preferred_element_type=jnp.float32)


def mm(a, b):
    return jnp.dot(a, b, preferred_element_type=jnp.float32)


def attention_kernel(rels, *refs):
    n = len(rels)
    choice, *q_hbm = refs[: 1 + n]
    k_own, k_oth, v_own, v_oth, o_ref, lse_ref = refs[1 + n : 7 + n]
    q_s, k_all, v_all, acc, m_s, l_s, r_s, mx_s, fresh, sems, q_sems = refs[7 + n :]
    scale = HD**-0.5 * LOG2E
    ctx = lax.axis_index("ctx")
    chip = ctx // 2
    core = lax.rem(ctx, 2)
    other = ctx + 1 - 2 * core
    q_copies = [
        pltpu.make_async_copy(q, q_s.at[pl.ds(i * CHUNK, CHUNK)], q_sems.at[i])
        for i, q in enumerate(q_hbm)
    ]
    for copy in q_copies:
        copy.start()
    for slot in range(SLOTS):
        src_k, src_v = (k_own, v_own) if slot < 2 else (k_oth, v_oth)
        src = pl.ds((slot % 2) * BLK, BLK)
        dst = pl.ds(slot * BLK, BLK)
        pltpu.make_async_copy(src_k.at[src], k_all.at[dst], sems.at[0, slot]).start()
        pltpu.make_async_copy(src_v.at[src], v_all.at[dst], sems.at[1, slot]).start()
    for copy in q_copies:
        copy.wait()
    ones = jnp.ones((BLK, HD), jnp.bfloat16)

    def queries(q0, i):
        return q_s[pl.ds(pl.multiple_of(q0 + i * SUB, SUB), SUB), :]

    def masked(s, first_key, first_query):
        key = first_key + lax.broadcasted_iota(jnp.int32, s.shape, 1)
        query = first_query + lax.broadcasted_iota(jnp.int32, s.shape, 0)
        return jnp.where(key <= query, s, LOW)

    def careful(q0, slot, first_key, steps, reach):
        @pl.loop(0, steps)
        def _(step):
            start = first_key + step * TKS
            at = pl.ds(pl.multiple_of(slot * BLK + start, TKS), TKS)
            for i in range(TQ // SUB):
                rows = pl.ds(i * SUB, SUB)
                s = masked(nt(queries(q0, i), k_all[at, :]) * scale, start, reach + i * SUB)
                old = m_s[rows]
                new = jnp.maximum(old, jnp.max(s, axis=1, keepdims=True))
                fade = jnp.exp2(old - new)
                p = jnp.exp2(s - new[:, :1])
                m_s[rows] = new
                l_s[rows] = l_s[rows] * fade + jnp.sum(p, axis=1, keepdims=True)
                acc[rows] = acc[rows] * fade + mm(p.astype(jnp.bfloat16), v_all[at, :])

    def quick(q0, slot, first_key, size, reach, mask):
        base = pl.multiple_of(slot * BLK + first_key, size)
        keys = k_all[pl.ds(base, size), :]
        vals = jnp.concatenate([v_all[pl.ds(base, size), :], ones[:size]], axis=1)
        for i in range(TQ // SUB):
            rows = pl.ds(i * SUB, SUB)
            s = nt(queries(q0, i), keys)
            if mask:
                s = masked(s, first_key, reach + i * SUB)
            old = m_s[rows]
            mx_s[rows] = jnp.broadcast_to(jnp.max(s, axis=1, keepdims=True) * scale, old.shape)
            p = jnp.exp2(s * scale - old[:, :1])
            r_s[rows] = mm(p.astype(jnp.bfloat16), vals)
        jump = jnp.max(mx_s[...] - m_s[...])

        @pl.when(jump <= JUMP)
        def _():
            old = m_s[...]
            new = jnp.maximum(old, mx_s[...])
            fade = jnp.exp2(old - new)
            m_s[...] = new
            acc[...] = (acc[...] + r_s[:, :HD]) * fade
            l_s[...] = (l_s[...] + r_s[:, HD:]) * fade

        @pl.when(jnp.logical_not(jump <= JUMP))
        def _():
            careful(q0, slot, first_key, size // TKS, reach)

    @pl.loop(0, n * CHUNK // TQ)
    def _(tile):
        q0 = pl.multiple_of(tile * TQ, TQ)
        chunk = lax.rem(chip + rels[0] + tile // (CHUNK // TQ), CHIPS)
        row = 14 + chunk // 2
        in_block = lax.rem(2 * chunk + core, 4) * CHUNK + lax.rem(tile, CHUNK // TQ) * TQ
        acc[...] = jnp.zeros_like(acc)
        l_s[...] = jnp.zeros_like(l_s)
        fresh[0] = 1

        @pl.loop(0, SLOTS)
        def _(slot):
            @pl.when(tile == 0)
            def _():
                at = pl.ds(pl.multiple_of(slot * BLK, BLK), BLK)
                first = pl.ds(0, BLK)
                pltpu.make_async_copy(k_own.at[first], k_all.at[at], sems.at[0, slot]).wait()
                pltpu.make_async_copy(v_own.at[first], v_all.at[at], sems.at[1, slot]).wait()

            block = jnp.where(slot < 2, 2 * ctx + slot, 2 * other + slot - 2)
            hit = choice[1, row] == block
            for j in range(2, 8):
                hit = jnp.logical_or(hit, choice[j, row] == block)
            own = block == row
            reach = jnp.where(own, in_block, BLK)

            @pl.when(jnp.logical_and(fresh[0] == 1, jnp.logical_or(own, hit)))
            def _():
                some = k_all[pl.ds(pl.multiple_of(slot * BLK, BLK), 256), :]
                s = masked(nt(q_s[pl.ds(q0, TQ), :], some) * scale, 0, reach)
                m_s[...] = jnp.broadcast_to(jnp.max(s, axis=1, keepdims=True), m_s.shape)
                fresh[0] = 0

            @pl.when(own)
            def _():
                last = in_block // TKS

                @pl.loop(0, last)
                def _(step):
                    quick(q0, slot, pl.multiple_of(step * TKS, TKS), TKS, reach, False)

                quick(q0, slot, pl.multiple_of(last * TKS, TKS), TKS, reach, True)

            @pl.when(jnp.logical_and(hit, jnp.logical_not(own)))
            def _():
                quick(q0, slot, 0, BLK, reach, False)

        total = l_s[...]
        some = total > 0.0
        total = jnp.where(some, total, 1.0)
        o_ref[pl.ds(q0, TQ), :] = (acc[...] / total).astype(jnp.bfloat16)
        lse = jnp.where(some, m_s[...] + jnp.log2(total), LOW)
        flat = jnp.transpose(lse)
        for i in range(TQ // HD):
            lse_ref[pl.ds(tile * (TQ // HD) + i, 1), :] = flat[:1, i * HD : (i + 1) * HD]


def attend(rels, choice, q_parts, k_own, k_oth, v_own, v_oth):
    n = len(rels)
    rows = n * CHUNK
    anywhere = pl.BlockSpec(memory_space=pl.ANY)
    vmem = pl.BlockSpec(memory_space=pltpu.VMEM)
    o, lse = pl.pallas_call(
        functools.partial(attention_kernel, rels),
        out_shape=[
            jax.ShapeDtypeStruct((rows, HD), jnp.bfloat16),
            jax.ShapeDtypeStruct((rows // HD, HD), jnp.float32),
        ],
        in_specs=[pl.BlockSpec(memory_space=pltpu.SMEM)] + [anywhere] * (4 + n),
        out_specs=[vmem, vmem],
        scratch_shapes=[
            pltpu.VMEM((rows, HD), jnp.bfloat16),
            pltpu.VMEM((SLOTS * BLK, HD), jnp.bfloat16),
            pltpu.VMEM((SLOTS * BLK, HD), jnp.bfloat16),
            pltpu.VMEM((TQ, HD), jnp.float32),
            pltpu.VMEM((TQ, HD), jnp.float32),
            pltpu.VMEM((TQ, HD), jnp.float32),
            pltpu.VMEM((TQ, 2 * HD), jnp.float32),
            pltpu.VMEM((TQ, HD), jnp.float32),
            pltpu.SMEM((1,), jnp.int32),
            pltpu.SemaphoreType.DMA((2, SLOTS)),
            pltpu.SemaphoreType.DMA((n,)),
        ],
        compiler_params=pltpu.CompilerParams(vmem_limit_bytes=60 * MIB),
        cost_estimate=pl.CostEstimate(
            flops=2 * 2 * rows * 2 * BLK * 2 * HD, bytes_accessed=10 * MIB, transcendentals=0
        ),
        name="attention_" + "_".join(str(rel) for rel in rels),
    )(choice, *q_parts, k_own, k_oth, v_own, v_oth)
    return o.reshape(n, CHUNK, HD), lse.reshape(n, CHUNK // HD, HD)


SIDE = 4
PACK = SIDE * CAP
LINE = SIDE * TOK
ROWS = EXPERTS * CAP
HALF = 1024
PART = 512
PARTS = HALF // PART
BACK = 512
BACKS = HALF // BACK
STEP = 256


def post_kernel(
    o0_ref, o_ref, lse0_ref, lse_ref, hid_ref, ids_ref, gain_ref, router_ref,
    proj_hbm, gate_hbm, up_hbm, down_hbm,
    out_ref,
    o_in, lse_in, ids_all, att, heads, proj, gate, up, down, wide, packs, place_t, turn,
    line, mixes, pick_out, pick_in, x_turned, sums, inner, turned, y_out, y_in, z_out, z_in,
    near, x_send, x_recv, i_send, i_recv, a_send, a_recv, l_send, l_recv, m_send, m_recv,
    p_send, p_recv, r_send, r_recv,
):
    ctx = lax.axis_index("ctx")
    me = lax.axis_index("exp")
    chip = ctx // 2
    core = lax.rem(ctx, 2)
    yy = me // SIDE
    zz = lax.rem(me, SIDE)
    width = hid_ref.shape[1]
    bf16 = jnp.bfloat16

    def along(axis, d):
        if axis == 0:
            return lax.rem(yy + d, SIDE) * SIDE + zz
        return yy * SIDE + lax.rem(zz + d, SIDE)

    firsts = (1, 0)
    seconds = (0, 1)
    at_first = (zz, yy)
    at_second = (yy, zz)

    loads = [
        pltpu.make_async_copy(src, dst, near.at[i])
        for i, (src, dst) in enumerate(
            ((proj_hbm, proj), (gate_hbm, gate), (up_hbm, up), (down_hbm, down))
        )
    ]
    for load in loads:
        load.start()
    barrier = pltpu.get_barrier_semaphore()
    for d in range(1, CHIPS):
        peer = (2 * lax.rem(chip + d, CHIPS) + core, me)
        pl.semaphore_signal(barrier, inc=1, device_id=peer, device_id_type=MESH)
    for d in range(1, EXPERTS):
        peer = (ctx, lax.rem(me + d, EXPERTS))
        pl.semaphore_signal(barrier, inc=1, device_id=peer, device_id_type=MESH)
    ids_all[me] = jnp.full((TOK, HD), -1, jnp.int32)
    own_ids = jnp.transpose(ids_ref[...].astype(jnp.float32)).astype(jnp.int32)
    ids_all[me, :, :6] = own_ids
    pl.semaphore_wait(barrier, CHIPS - 1 + EXPERTS - 1)

    def remote(src, dst, send, recv, peer):
        copy = pltpu.make_async_remote_copy(
            src_ref=src, dst_ref=dst, send_sem=send, recv_sem=recv,
            device_id=peer, device_id_type=MESH,
        )
        copy.start()
        return copy

    i_copies = []
    for d in range(1, EXPERTS):
        peer = (ctx, lax.rem(me + d, EXPERTS))
        i_copies.append(
            remote(ids_all.at[me], ids_all.at[me], i_send.at[d - 1], i_recv.at[d - 1], peer)
        )
    x_copies = []
    for d in (2, 1, 3):
        peer = (2 * lax.rem(chip + d, CHIPS) + core, me)
        for kind, src, dst in ((0, o_ref, o_in), (1, lse_ref, lse_in)):
            x_copies.append(
                remote(
                    src.at[d - 1], dst.at[d - 1], x_send.at[kind, d - 1], x_recv.at[kind, d - 1],
                    peer,
                )
            )
    to_row = lax.broadcasted_iota(jnp.int32, (ROWS, HD), 0)
    owner = to_row // CAP
    source = (lax.rem(owner, SIDE) * SIDE + owner // SIDE) * CAP + lax.rem(to_row, CAP)
    from_row = lax.broadcasted_iota(jnp.int32, (ROWS, ROWS), 1)
    turn[...] = jnp.where(from_row == source[:, :1], 1.0, 0.0).astype(bf16)
    for copy in i_copies:
        copy.wait()
    t_to = lax.broadcasted_iota(jnp.int32, (LINE, LINE), 0)
    t_from = lax.broadcasted_iota(jnp.int32, (LINE, LINE), 1)
    before = jnp.where((t_from < t_to) & (t_from // TOK == t_to // TOK), 1.0, 0.0).astype(bf16)
    base = ((lax.broadcasted_iota(jnp.int32, (LINE, HD), 0) // TOK) * CAP).astype(jnp.float32)
    lane = lax.broadcasted_iota(jnp.int32, (LINE, HD), 1)
    slot = lax.broadcasted_iota(jnp.int32, (LINE, LINE), 1).astype(jnp.float32)
    slot_t = lax.broadcasted_iota(jnp.int32, (PACK, LINE), 0).astype(jnp.float32)
    for half in range(2):
        owners = [yy * SIDE + i if half == 0 else i * SIDE + zz for i in range(SIDE)]
        ids = jnp.concatenate([ids_all[owner] for owner in owners], axis=0)
        chosen = functools.reduce(jnp.logical_or, [ids[:, j : j + 1] == lane for j in range(6)])
        rank = mm(before, jnp.where(chosen, 1.0, 0.0).astype(bf16))
        place = jnp.where(chosen, base + rank, -1.0)
        place_t[half] = jnp.transpose(place)
        for d in range(SIDE):
            expert = along(seconds[half], d)
            column = jnp.sum(jnp.where(lane == expert, place, 0.0), axis=1, keepdims=True)
            packs[half, d] = jnp.where(slot == column, 1.0, 0.0).astype(bf16)

    for copy in x_copies:
        copy.wait()
    parts = [lse0_ref[0]] + [lse_in[d] for d in range(CHIPS - 1)]
    top = functools.reduce(jnp.maximum, parts)
    weights = [jnp.exp2(part - top) for part in parts]
    total = functools.reduce(jnp.add, weights)
    columns = [jnp.transpose(weight / total) for weight in weights]
    for g in range(CHUNK // HD):
        rows = pl.ds(g * HD, HD)
        mixed = columns[0][:, g : g + 1] * o0_ref[0, rows, :].astype(jnp.float32)
        for d in range(CHIPS - 1):
            mixed += columns[d + 1][:, g : g + 1] * o_in[d, rows, :].astype(jnp.float32)
        att[2 * g] = mixed[:TOK].astype(bf16)
        att[2 * g + 1] = mixed[TOK:].astype(bf16)
    a_copies = []
    for d in range(1, EXPERTS):
        to = lax.rem(me + d, EXPERTS)
        a_copies.append(
            remote(att.at[to], heads.at[me], a_send.at[d - 1], a_recv.at[d - 1], (ctx, to))
        )
    heads[me] = att[me]

    loads[0].wait()
    for copy in a_copies:
        copy.wait()
    joined = jnp.concatenate([heads[h] for h in range(EXPERTS)], axis=1)

    @pl.loop(0, width // STEP)
    def _(c):
        cols = pl.ds(pl.multiple_of(c * STEP, STEP), STEP)
        wide[:, cols] = hid_ref[:, cols].astype(jnp.float32) + mm(joined, proj[:, cols])

    residual = wide[...].astype(bf16).astype(jnp.float32)
    wide[...] = residual
    square = jnp.mean(residual * residual, axis=1, keepdims=True)
    normed = (residual * lax.rsqrt(square + NORM_EPS) * gain_ref[...]).astype(bf16)

    l_copies = {}
    for part in range(PARTS):
        for half in range(2):
            start = half * HALF + part * PART
            line[half, part, at_first[half]] = normed[:, start : start + PART]
            view = line.at[half, part, at_first[half]]
            for d in (2, 1, 3):
                l_copies[half, part, d] = remote(
                    view, view, l_send.at[half, part, d - 1], l_recv.at[half, part, d - 1],
                    (ctx, along(firsts[half], d)),
                )
    affinity = jax.nn.sigmoid(nt(normed, router_ref[...]))
    expert_lane = lax.broadcasted_iota(jnp.int32, affinity.shape, 1)
    chosen = functools.reduce(
        jnp.logical_or, [own_ids[:, j : j + 1] == expert_lane for j in range(6)]
    )
    picked = jnp.where(chosen, affinity, 0.0)
    mix = ROUTE_SCALE * picked / jnp.sum(picked, axis=1, keepdims=True)
    for half in range(2):
        mixes[half, at_first[half]] = jnp.zeros((TOK, HD), jnp.float32)
        mixes[half, at_first[half], :, :EXPERTS] = mix
    p_copies = {}
    for part in range(PARTS):
        for half in range(2):
            for d in (1, 3, 2):
                l_copies[half, part, d].wait_recv()
            mine = pl.ds(pl.multiple_of(at_second[half] * PACK, PACK), PACK)
            tokens = jnp.concatenate([line[half, part, i] for i in range(SIDE)], axis=0)
            for d in (2, 1, 3, 0):
                expert = along(seconds[half], d)
                row = place_t[half, pl.ds(expert, 1), :]
                rows = mm(jnp.where(slot_t == row, 1.0, 0.0).astype(bf16), tokens).astype(bf16)
                if d == 0:
                    pick_in[half, part, mine, :] = rows
                else:
                    pick_out[half, part, d - 1] = rows
                    p_copies[half, part, d] = remote(
                        pick_out.at[half, part, d - 1], pick_in.at[half, part, mine],
                        p_send.at[half, part, d - 1], p_recv.at[half, part, d - 1], (ctx, expert),
                    )
    m_copies = []
    for half in range(2):
        for d in (2, 1, 3):
            view = mixes.at[half, at_first[half]]
            m_copies.append(
                remote(
                    view, view, m_send.at[half, d - 1], m_recv.at[half, d - 1],
                    (ctx, along(firsts[half], d)),
                )
            )
    loads[1].wait()
    loads[2].wait()
    units = gate.shape[1]
    for part in range(PARTS):
        for half in (1, 0):
            for d in (1, 3, 2):
                p_copies[half, part, d].wait_recv()
            if half == 1:
                x_turned[...] = mm(turn[...], pick_in[1, part]).astype(bf16)
        low = pl.ds(part * PART, PART)
        high = pl.ds(HALF + part * PART, PART)
        for start in range(0, units, STEP):
            cols = slice(start, min(start + STEP, units))
            gated = mm(pick_in[0, part], gate[low, cols]) + mm(x_turned[...], gate[high, cols])
            raised = mm(pick_in[0, part], up[low, cols]) + mm(x_turned[...], up[high, cols])
            if part > 0:
                gated += sums[0, :, cols]
                raised += sums[1, :, cols]
            if part < PARTS - 1:
                sums[0, :, cols] = gated
                sums[1, :, cols] = raised
            else:
                inner[:, cols] = (gated / (1.0 + jnp.exp(-gated)) * raised).astype(bf16)
    turned[...] = mm(turn[...], inner[...]).astype(bf16)
    loads[3].wait()
    r_copies = {}
    for part in range(BACKS):
        for half in range(2):
            rows_in = inner if half == 0 else turned

            @pl.loop(0, BACK // STEP)
            def _(c):
                cols = pl.ds(pl.multiple_of(c * STEP, STEP), STEP)
                from_cols = pl.ds(pl.multiple_of(half * HALF + part * BACK + c * STEP, STEP), STEP)
                y_out[half, part, :, cols] = mm(rows_in[...], down[:, from_cols]).astype(bf16)

            for d in (2, 1, 3):
                to = lax.rem(at_second[half] + d, SIDE)
                r_copies[half, part, 0, d] = remote(
                    y_out.at[half, part, pl.ds(pl.multiple_of(to * PACK, PACK), PACK)],
                    y_in.at[half, part, d - 1],
                    r_send.at[half, part, 0, d - 1], r_recv.at[half, part, 0, d - 1],
                    (ctx, along(seconds[half], d)),
                )

    for copy in m_copies:
        copy.wait_recv()
    for part in range(BACKS):
        for half in range(2):
            here = at_second[half]
            share_of = jnp.concatenate([mixes[half, i] for i in range(SIDE)], axis=0)
            summed = jnp.zeros((LINE, BACK), jnp.float32)
            for d in (0, 1, 3, 2):
                back = (SIDE - d) % SIDE
                expert = along(seconds[half], back)
                column = jnp.sum(jnp.where(lane == expert, share_of, 0.0), axis=1, keepdims=True)
                if d == 0:
                    rows = y_out[half, part, pl.ds(pl.multiple_of(here * PACK, PACK), PACK), :]
                else:
                    r_copies[half, part, 0, d].wait_recv()
                    rows = y_in[half, part, d - 1]
                summed += column * mm(packs[half, back][:, :PACK], rows)
            for i in range(SIDE):
                z_out[half, part, i] = summed[i * TOK : (i + 1) * TOK].astype(bf16)
            for d in (2, 1, 3):
                r_copies[half, part, 1, d] = remote(
                    z_out.at[half, part, lax.rem(at_first[half] + d, SIDE)],
                    z_in.at[half, part, d - 1],
                    r_send.at[half, part, 1, d - 1], r_recv.at[half, part, 1, d - 1],
                    (ctx, along(firsts[half], d)),
                )
    for part in range(BACKS):
        for half in range(2):
            start = half * HALF + part * BACK
            cols = slice(start, start + BACK)
            result = wide[:, cols] + z_out[half, part, at_first[half]].astype(jnp.float32)
            for d in (1, 3, 2):
                r_copies[half, part, 1, d].wait_recv()
                result += z_in[half, part, d - 1].astype(jnp.float32)
            out_ref[:, cols] = result.astype(bf16)
    for group in (l_copies, p_copies, r_copies):
        for copy in group.values():
            copy.wait_send()
    for copy in m_copies:
        copy.wait_send()


def post(o0, o, lse0, lse, hidden_in, ids_t, gain, router_t, proj, w_gate, w_up, w_down):
    width = hidden_in.shape[1]
    units = w_gate.shape[1]
    anywhere = pl.BlockSpec(memory_space=pl.ANY)
    vmem = pl.BlockSpec(memory_space=pltpu.VMEM)
    bf16 = jnp.bfloat16
    f32 = jnp.float32
    dma = pltpu.SemaphoreType.DMA
    others = SIDE - 1
    return pl.pallas_call(
        post_kernel,
        out_shape=jax.ShapeDtypeStruct((TOK, width), bf16),
        in_specs=[vmem] * 8 + [anywhere] * 4,
        out_specs=vmem,
        scratch_shapes=[
            pltpu.VMEM((CHIPS - 1, CHUNK, HD), bf16),
            pltpu.VMEM((CHIPS - 1, CHUNK // HD, HD), f32),
            pltpu.VMEM((EXPERTS, TOK, HD), jnp.int32),
            pltpu.VMEM((EXPERTS, TOK, HD), bf16),
            pltpu.VMEM((EXPERTS, TOK, HD), bf16),
            pltpu.VMEM((width, width), bf16),
            pltpu.VMEM((width, units), bf16),
            pltpu.VMEM((width, units), bf16),
            pltpu.VMEM((units, width), bf16),
            pltpu.VMEM((TOK, width), f32),
            pltpu.VMEM((2, SIDE, LINE, LINE), bf16),
            pltpu.VMEM((2, HD, LINE), f32),
            pltpu.VMEM((ROWS, ROWS), bf16),
            pltpu.VMEM((2, PARTS, SIDE, TOK, PART), bf16),
            pltpu.VMEM((2, SIDE, TOK, HD), f32),
            pltpu.VMEM((2, PARTS, others, PACK, PART), bf16),
            pltpu.VMEM((2, PARTS, ROWS, PART), bf16),
            pltpu.VMEM((ROWS, PART), bf16),
            pltpu.VMEM((2, ROWS, units), f32),
            pltpu.VMEM((ROWS, units), bf16),
            pltpu.VMEM((ROWS, units), bf16),
            pltpu.VMEM((2, BACKS, ROWS, BACK), bf16),
            pltpu.VMEM((2, BACKS, others, PACK, BACK), bf16),
            pltpu.VMEM((2, BACKS, SIDE, TOK, BACK), bf16),
            pltpu.VMEM((2, BACKS, others, TOK, BACK), bf16),
            dma((4,)),
            dma((2, CHIPS - 1)),
            dma((2, CHIPS - 1)),
            dma((EXPERTS - 1,)),
            dma((EXPERTS - 1,)),
            dma((EXPERTS - 1,)),
            dma((EXPERTS - 1,)),
            dma((2, PARTS, others)),
            dma((2, PARTS, others)),
            dma((2, others)),
            dma((2, others)),
            dma((2, PARTS, others)),
            dma((2, PARTS, others)),
            dma((2, BACKS, 2, others)),
            dma((2, BACKS, 2, others)),
        ],
        compiler_params=pltpu.CompilerParams(
            collective_id=1, has_side_effects=True, vmem_limit_bytes=62 * MIB
        ),
        name="post",
    )(o0, o, lse0, lse, hidden_in, ids_t, gain, router_t, proj, w_gate, w_up, w_down)


def local(
    hidden_in, queries, keys, values, block_choice, out_proj, norm_gain, router, expert_ids,
    w_gate, w_up, w_down,
):
    width = hidden_in.shape[1]
    proj_all = lax.all_gather(out_proj, "exp", axis=0, tiled=True)
    devices = range(2 * CHIPS)
    swap = [(i, i ^ 1) for i in devices]
    k_oth = lax.ppermute(keys, "ctx", swap)
    v_oth = lax.ppermute(values, "ctx", swap)
    q_from = [
        lax.ppermute(queries, "ctx", [(i, (i - 2 * d) % (2 * CHIPS)) for i in devices])
        for d in range(1, CHIPS)
    ]
    blocks = (keys, k_oth, values, v_oth)
    choice = block_choice.T
    o0, lse0 = attend((0,), choice, (queries,), *blocks)
    o0, *q_from = lax.optimization_barrier((o0, *q_from))
    o, lse = attend((1, 2, 3), choice, q_from, *blocks)
    return post(
        o0, o, lse0, lse, hidden_in, expert_ids.T, norm_gain.reshape(1, width), router.T,
        proj_all, w_gate[0], w_up[0], w_down[0],
    )


def solution(mesh):
    placed = (
        P(("ctx", "exp"), None),
        P("ctx", "exp"),
        P("ctx", "exp"),
        P("ctx", "exp"),
        P(),
        P("exp", None),
        P(),
        P(),
        P(("ctx", "exp"), None),
        P("exp", None, None),
        P("exp", None, None),
        P("exp", None, None),
    )
    return jax.shard_map(
        local, mesh=mesh, in_specs=placed, out_specs=P(("ctx", "exp"), None), check_vma=False
    )
```

time: 203 us -> 184 us (0.906)
  the two profiles are of different devices: /device:TPU:1 before, /device:TPU:0 now
where the time goes in v3:
time: 184 us
  Pallas kernels  149 us (81%)
  between operations  13.5 us (7%)
  waiting for transfers between devices  13.4 us (7%)
  starting transfers between devices  5.11 us (3%)
  local copies, waits for them, and re-layouts  2.8 us (2%)
    pallas_call x1, Pallas kernels, post(): pl.pallas_call(post_kernel, out_shape=jax.ShapeDtypeStruct((TOK, width),...  92.3 us
    pallas_call x2, Pallas kernels, attend(): pl.pallas_call(functools.partial(attention_kernel, rels), out_shape=[jax....  56.6 us
    all_gather x1, waiting for transfers between devices, local(): proj_all = lax.all_gather(out_proj, 'exp', axis=0, tiled=True)  10.2 us
    ppermute x3, starting transfers between devices, local(): lax.ppermute(queries, 'ctx', [(i, (i - 2 * d) % (2 * CHIPS)) for i in dev...  4.53 us
  transfers between devices with their start and end apart: 6, of which 3 were waited for; matrix products, arithmetic and copies ran while one was open for 0% of the time, Pallas kernels for 31%

profile of v3, /device:TPU:0, one launch (start us, length us, event | category | flops | bytes accessed | tf_op | source)
XLA Modules:
  0.0 183.7 jit_solution(69835644134708112)
XLA Ops:
  6.5 0.0 all-gather.2.cloned.1.call-start
  6.5 0.7 all-gather.2.cloned.1.call-update
  7.3 0.1 collective-permute-start
  7.4 0.5 collective-permute-start.1
  7.8 2.8 %collective-permute-start.2 = (bf16[1024,128]{1,0:T(8,128)(2,1)}, bf16[1024,128]{1,0:T(8,128)(2,1)S(1)}, u32[]{:S(2)}, u32[]{:S(2)}) collective-permute-start(bf16[1024,128]{1,0:T(8,128)(2,1)} %refs_1_.1), channel_id=1, source_target_pairs={{0,96},{16,112},{32,0},{48,16},{64,32},{80,48},{96,64},{112,80},{1... | collective-permute-start | bytes 786440 | tf_op jit(solution)/shard_map/ppermute | solution.py:568
  10.7 0.8 collective-permute-start.3
  11.5 0.9 collective-permute-start.4
  12.4 1.4 collective-permute-done.refs_3_.refs_5_
  13.8 0.0 copy-start
  13.8 1.1 collective-permute-done.1.refs_5_.refs_7_
  14.8 0.3 copy-done
  15.1 16.3 %attention_0.1 = (bf16[1024,128]{1,0:T(8,128)(2,1)}, f32[8,128]{1,0:T(8,128)}) custom-call(s32[8,16]{1,0:T(8,128)} %bitcast.21, bf16[1024,128]{1,0:T(8,128)(2,1)} %refs_1_.1, bf16[8192,128]{1,0:T(8,128)(2,1)} %refs_4_.3, bf16[8192,128]{1,0:T(8,128)(2,1)} %copy-done, bf16[8192,128]{1,0:T(8,128)(2,1)} %refs_6_.1, ...), custom_call_target="tpu_custom_call" | custom-call | flops 8589934592 | bytes 10485760 | tf_op jit(solution)/shard_map/attention_0/pallas_call | solution.py:180
  31.4 0.0 collective-permute-done.2.refs_1_
  31.4 0.0 copy-start.1
  31.4 0.0 collective-permute-done.3.refs_2_
  31.5 0.0 copy-start.2
  31.5 0.0 collective-permute-done.4.refs_3_
  31.5 0.0 copy-start.3
  31.5 0.7 copy-done.1
  32.1 0.1 copy-done.2
  32.2 0.1 copy-done.3
  32.3 40.3 %attention_1_2_3.1 = (bf16[3072,128]{1,0:T(8,128)(2,1)}, f32[24,128]{1,0:T(8,128)}) custom-call(s32[8,16]{1,0:T(8,128)} %bitcast.22, bf16[1024,128]{1,0:T(8,128)(2,1)} %copy-done.1, bf16[1024,128]{1,0:T(8,128)(2,1)} %copy-done.2, bf16[1024,128]{1,0:T(8,128)(2,1)} %copy-done.3, bf16[8192,128]{1,0:T(8,128)(2,1)} %refs_4_.3, bf16[8192,128]{1,0:T(8,128)(2,1)} %copy-done, ...), custom_call_target="tpu_custom_call" | custom-call | flops 25769803776 | bytes 10485760 | tf_op jit(solution)/shard_map/attention_1_2_3/pallas_call | solution.py:180
  72.7 10.2 %all-gather.2.cloned.1.call-done.proj_hbm = bf16[2048,2048]{1,0:T(8,128)(2,1)} async-done(((bf16[128,2048]{1,0:T(8,128)(2,1)}), bf16[2048,2048]{1,0:T(8,128)(2,1)}) %all-gather.2.cloned.1.call-update) | async-done | bytes 8388624 | tf_op jit(solution)/shard_map/all_gather | solution.py:562
  82.8 92.3 %post.1 = bf16[64,2048]{1,0:T(8,128)(2,1)} custom-call(bf16[1,1024,128]{2,1,0:T(8,128)(2,1)} %bitcast.15, bf16[3,1024,128]{2,1,0:T(8,128)(2,1)} %bitcast.14, f32[1,8,128]{2,1,0:T(8,128)} %bitcast.20, f32[3,8,128]{2,1,0:T(8,128)} %bitcast.17, bf16[64,2048]{1,0:T(8,128)(2,1)} %hid_ref.1, s32[6,64]{1,0:T(8,128)} %bitcast.19, f32[1,2048]{1,0:T(1,128)} %bitcast.18, ...), custom_call_target="tpu_custom_call" | custom-call | tf_op jit(solution)/shard_map/post/pallas_call | solution.py:503
  175.2 1.7 copy.14
Async XLA Ops:
  6.5 76.3 %all-gather.2.cloned.1.call-start = ((), (), s32[]{:S(2)}) async-start(), calls=%async_computation | async-start | bytes 8912896 | tf_op jit(solution)/shard_map/all_gather | solution.py:562
  7.3 6.5 %collective-permute-start = (bf16[8192,128]{1,0:T(8,128)(2,1)}, bf16[8192,128]{1,0:T(8,128)(2,1)S(1)}, u32[]{:S(2)}, u32[]{:S(2)}) collective-permute-start(bf16[8192,128]{1,0:T(8,128)(2,1)} %refs_4_.3), channel_id=1, source_target_pairs={{0,16},{16,0},{32,48},{48,32},{64,80},{80,64},{96,112},{112,96},{1... | collective-permute-start | bytes 6291464 | tf_op jit(solution)/shard_map/ppermute | solution.py:565
  7.4 7.5 %collective-permute-start.1 = (bf16[8192,128]{1,0:T(8,128)(2,1)}, bf16[8192,128]{1,0:T(8,128)(2,1)}, u32[]{:S(2)}, u32[]{:S(2)}) collective-permute-start(bf16[8192,128]{1,0:T(8,128)(2,1)} %refs_6_.1), channel_id=1, source_target_pairs={{0,16},{16,0},{32,48},{48,32},{64,80},{80,64},{96,112},{112,96},{1... | collective-permute-start | bytes 6291464 | tf_op jit(solution)/shard_map/ppermute | solution.py:566
  7.8 23.6 %collective-permute-start.2 = (bf16[1024,128]{1,0:T(8,128)(2,1)}, bf16[1024,128]{1,0:T(8,128)(2,1)S(1)}, u32[]{:S(2)}, u32[]{:S(2)}) collective-permute-start(bf16[1024,128]{1,0:T(8,128)(2,1)} %refs_1_.1), channel_id=1, source_target_pairs={{0,96},{16,112},{32,0},{48,16},{64,32},{80,48},{96,64},{112,80},{1... | collective-permute-start | bytes 786440 | tf_op jit(solution)/shard_map/ppermute | solution.py:568
  10.7 20.8 %collective-permute-start.3 = (bf16[1024,128]{1,0:T(8,128)(2,1)}, bf16[1024,128]{1,0:T(8,128)(2,1)S(1)}, u32[]{:S(2)}, u32[]{:S(2)}) collective-permute-start(bf16[1024,128]{1,0:T(8,128)(2,1)} %refs_1_.1), channel_id=1, source_target_pairs={{0,64},{16,80},{32,96},{48,112},{64,0},{80,16},{96,32},{112,48},{1... | collective-permute-start | bytes 786440 | tf_op jit(solution)/shard_map/ppermute | solution.py:568
  11.5 20.0 %collective-permute-start.4 = (bf16[1024,128]{1,0:T(8,128)(2,1)}, bf16[1024,128]{1,0:T(8,128)(2,1)S(1)}, u32[]{:S(2)}, u32[]{:S(2)}) collective-permute-start(bf16[1024,128]{1,0:T(8,128)(2,1)} %refs_1_.1), channel_id=1, source_target_pairs={{0,32},{16,48},{32,64},{48,80},{64,96},{80,112},{96,0},{112,16},{1... | collective-permute-start | bytes 786440 | tf_op jit(solution)/shard_map/ppermute | solution.py:568
  13.8 1.4 copy-start
  31.4 0.7 copy-start.1
  31.5 0.8 copy-start.2
  31.5 0.9 copy-start.3
Sparse Core Ops, SparseCore 0:
  9.5 73.2 all-gather.1

commit v4 on v3

--- a/solution.py
+++ b/solution.py
@@ -223,9 +223,9 @@
     o0_ref, o_ref, lse0_ref, lse_ref, hid_ref, ids_ref, gain_ref, router_ref,
     proj_hbm, gate_hbm, up_hbm, down_hbm,
     out_ref,
-    o_in, lse_in, ids_all, att, heads, proj, gate, up, down, wide, packs, place_t, turn,
+    o_in, lse_in, mixing, ids_all, att, heads, proj, gate, up, down, wide, packs, place_t, turn,
     line, mixes, pick_out, pick_in, x_turned, sums, inner, turned, y_out, y_in, z_out, z_in,
-    near, x_send, x_recv, i_send, i_recv, a_send, a_recv, l_send, l_recv, m_send, m_recv,
+    near, w_send, w_recv, x_send, x_recv, i_send, i_recv, a_send, a_recv, l_send, l_recv, m_send, m_recv,
     p_send, p_recv, r_send, r_recv,
 ):
     ctx = lax.axis_index("ctx")
@@ -281,23 +281,26 @@
         i_copies.append(
             remote(ids_all.at[me], ids_all.at[me], i_send.at[d - 1], i_recv.at[d - 1], peer)
         )
-    x_copies = []
-    for d in (2, 1, 3):
-        peer = (2 * lax.rem(chip + d, CHIPS) + core, me)
-        for kind, src, dst in ((0, o_ref, o_in), (1, lse_ref, lse_in)):
-            x_copies.append(
-                remote(
-                    src.at[d - 1], dst.at[d - 1], x_send.at[kind, d - 1], x_recv.at[kind, d - 1],
-                    peer,
-                )
+    w_copies = [
+        remote(
+            lse_ref.at[d - 1], lse_in.at[d - 1], w_send.at[d - 1], w_recv.at[d - 1],
+            (2 * lax.rem(chip + d, CHIPS) + core, me),
+        )
+        for d in (2, 1, 3)
+    ]
+    x_copies = {}
+    for k in range(SIDE):
+        rows = pl.ds(pl.multiple_of(lax.rem(yy + k, SIDE) * LINE, LINE), LINE)
+        for d in (2, 1, 3):
+            x_copies[k, d] = remote(
+                o_ref.at[d - 1, rows], o_in.at[d - 1, rows], x_send.at[k, d - 1],
+                x_recv.at[k, d - 1], (2 * lax.rem(chip + d, CHIPS) + core, me),
             )
     to_row = lax.broadcasted_iota(jnp.int32, (ROWS, HD), 0)
     owner = to_row // CAP
     source = (lax.rem(owner, SIDE) * SIDE + owner // SIDE) * CAP + lax.rem(to_row, CAP)
     from_row = lax.broadcasted_iota(jnp.int32, (ROWS, ROWS), 1)
     turn[...] = jnp.where(from_row == source[:, :1], 1.0, 0.0).astype(bf16)
-    for copy in i_copies:
-        copy.wait()
     t_to = lax.broadcasted_iota(jnp.int32, (LINE, LINE), 0)
     t_from = lax.broadcasted_iota(jnp.int32, (LINE, LINE), 1)
     before = jnp.where((t_from < t_to) & (t_from // TOK == t_to // TOK), 1.0, 0.0).astype(bf16)
@@ -305,7 +308,7 @@
     lane = lax.broadcasted_iota(jnp.int32, (LINE, HD), 1)
     slot = lax.broadcasted_iota(jnp.int32, (LINE, LINE), 1).astype(jnp.float32)
     slot_t = lax.broadcasted_iota(jnp.int32, (PACK, LINE), 0).astype(jnp.float32)
-    for half in range(2):
+    def pack(half):
         owners = [yy * SIDE + i if half == 0 else i * SIDE + zz for i in range(SIDE)]
         ids = jnp.concatenate([ids_all[owner] for owner in owners], axis=0)
         chosen = functools.reduce(jnp.logical_or, [ids[:, j : j + 1] == lane for j in range(6)])
@@ -317,27 +320,40 @@
             column = jnp.sum(jnp.where(lane == expert, place, 0.0), axis=1, keepdims=True)
             packs[half, d] = jnp.where(slot == column, 1.0, 0.0).astype(bf16)
 
-    for copy in x_copies:
+
+    for copy in w_copies:
         copy.wait()
     parts = [lse0_ref[0]] + [lse_in[d] for d in range(CHIPS - 1)]
     top = functools.reduce(jnp.maximum, parts)
     weights = [jnp.exp2(part - top) for part in parts]
     total = functools.reduce(jnp.add, weights)
-    columns = [jnp.transpose(weight / total) for weight in weights]
-    for g in range(CHUNK // HD):
-        rows = pl.ds(g * HD, HD)
-        mixed = columns[0][:, g : g + 1] * o0_ref[0, rows, :].astype(jnp.float32)
-        for d in range(CHIPS - 1):
-            mixed += columns[d + 1][:, g : g + 1] * o_in[d, rows, :].astype(jnp.float32)
-        att[2 * g] = mixed[:TOK].astype(bf16)
-        att[2 * g + 1] = mixed[TOK:].astype(bf16)
+    for d in range(CHIPS):
+        column = jnp.transpose(weights[d] / total)
+        for g in range(CHUNK // HD):
+            mixing[d, g * HD : (g + 1) * HD] = jnp.broadcast_to(column[:, g : g + 1], (HD, HD))
     a_copies = []
-    for d in range(1, EXPERTS):
-        to = lax.rem(me + d, EXPERTS)
-        a_copies.append(
-            remote(att.at[to], heads.at[me], a_send.at[d - 1], a_recv.at[d - 1], (ctx, to))
-        )
-    heads[me] = att[me]
+    for k in range(SIDE):
+        for d in (1, 3, 2):
+            x_copies[k, d].wait()
+        for i in range(SIDE):
+            to = lax.rem(yy + k, SIDE) * SIDE + lax.rem(zz + i, SIDE)
+            rows = pl.ds(pl.multiple_of(to * TOK, TOK), TOK)
+            mixed = mixing[0, rows, :] * o0_ref[0, rows, :].astype(jnp.float32)
+            for d in range(CHIPS - 1):
+                mixed += mixing[d + 1, rows, :] * o_in[d, rows, :].astype(jnp.float32)
+            if k == 0 and i == 0:
+                heads[me] = mixed.astype(bf16)
+            else:
+                n = k * SIDE + i - 1
+                att[to] = mixed.astype(bf16)
+                a_copies.append(
+                    remote(att.at[to], heads.at[me], a_send.at[n], a_recv.at[n], (ctx, to))
+                )
+        if k == 0:
+            for copy in i_copies:
+                copy.wait()
+        if k < 2:
+            pack(k)
 
     loads[0].wait()
     for copy in a_copies:
@@ -508,6 +524,7 @@
         scratch_shapes=[
             pltpu.VMEM((CHIPS - 1, CHUNK, HD), bf16),
             pltpu.VMEM((CHIPS - 1, CHUNK // HD, HD), f32),
+            pltpu.VMEM((CHIPS, CHUNK, HD), f32),
             pltpu.VMEM((EXPERTS, TOK, HD), jnp.int32),
             pltpu.VMEM((EXPERTS, TOK, HD), bf16),
             pltpu.VMEM((EXPERTS, TOK, HD), bf16),
@@ -532,8 +549,10 @@
             pltpu.VMEM((2, BACKS, SIDE, TOK, BACK), bf16),
             pltpu.VMEM((2, BACKS, others, TOK, BACK), bf16),
             dma((4,)),
-            dma((2, CHIPS - 1)),
-            dma((2, CHIPS - 1)),
+            dma((CHIPS - 1,)),
+            dma((CHIPS - 1,)),
+            dma((SIDE, CHIPS - 1)),
+            dma((SIDE, CHIPS - 1)),
             dma((EXPERTS - 1,)),
             dma((EXPERTS - 1,)),
             dma((EXPERTS - 1,)),

time: 184 us -> 177 us (0.962)
  waiting for transfers between devices: 13.4 us -> 3.2 us
  Pallas kernels: 149 us -> 152 us
    pallas_call x2, Pallas kernels: 56.6 us -> 74.3 us  [attend(): pl.pallas_call(functools.partial(attention_kernel, rels), out_shape=[jax....]
    pallas_call x1, Pallas kernels: 92.3 us -> 77.7 us  [post(): pl.pallas_call(post_kernel, out_shape=jax.ShapeDtypeStruct((TOK, width),...]
    all_gather x1, waiting for transfers between devices: 10.2 us -> 0.02 us  [local(): proj_all = lax.all_gather(out_proj, 'exp', axis=0, tiled=True)]
  transfers between devices with their start and end apart: 6 -> 6, of which waited for: 3 -> 2; matrix products, arithmetic and copies ran while one was open for 0% -> 0% of each run, Pallas kernels for 31% -> 42%
where the time goes in v4:
time: 177 us
  Pallas kernels  152 us (86%)
  between operations  13.5 us (8%)
  starting transfers between devices  5.11 us (3%)
  waiting for transfers between devices  3.2 us (2%)
  local copies, waits for them, and re-layouts  2.8 us (2%)
    pallas_call x1, Pallas kernels, post(): pl.pallas_call(post_kernel, out_shape=jax.ShapeDtypeStruct((TOK, width),...  77.7 us
    pallas_call x2, Pallas kernels, attend(): pl.pallas_call(functools.partial(attention_kernel, rels), out_shape=[jax....  74.3 us
    ppermute x3, starting transfers between devices, local(): lax.ppermute(queries, 'ctx', [(i, (i - 2 * d) % (2 * CHIPS)) for i in dev...  4.53 us
  transfers between devices with their start and end apart: 6, of which 2 were waited for; matrix products, arithmetic and copies ran while one was open for 0% of the time, Pallas kernels for 42%

profile of v4, /device:TPU:0, one launch (start us, length us, event | category | flops | bytes accessed | tf_op | source)
XLA Modules:
  0.0 176.6 jit_solution(10194096124066302086)
XLA Ops:
  6.5 0.0 all-gather.2.cloned.1.call-start
  6.5 0.7 all-gather.2.cloned.1.call-update
  7.3 0.1 collective-permute-start
  7.4 0.5 collective-permute-start.1
  7.8 2.8 %collective-permute-start.2 = (bf16[1024,128]{1,0:T(8,128)(2,1)}, bf16[1024,128]{1,0:T(8,128)(2,1)S(1)}, u32[]{:S(2)}, u32[]{:S(2)}) collective-permute-start(bf16[1024,128]{1,0:T(8,128)(2,1)} %refs_1_.1), channel_id=1, source_target_pairs={{0,96},{16,112},{32,0},{48,16},{64,32},{80,48},{96,64},{112,80},{1... | collective-permute-start | bytes 786440 | tf_op jit(solution)/shard_map/ppermute | solution.py:587
  10.7 0.8 collective-permute-start.3
  11.5 0.9 collective-permute-start.4
  12.4 1.4 collective-permute-done.refs_3_.refs_5_
  13.8 0.0 copy-start
  13.8 1.1 collective-permute-done.1.refs_5_.refs_7_
  14.8 0.3 copy-done
  15.1 21.6 %attention_0.1 = (bf16[1024,128]{1,0:T(8,128)(2,1)}, f32[8,128]{1,0:T(8,128)}) custom-call(s32[8,16]{1,0:T(8,128)} %bitcast.21, bf16[1024,128]{1,0:T(8,128)(2,1)} %refs_1_.1, bf16[8192,128]{1,0:T(8,128)(2,1)} %refs_4_.3, bf16[8192,128]{1,0:T(8,128)(2,1)} %copy-done, bf16[8192,128]{1,0:T(8,128)(2,1)} %refs_6_.1, ...), custom_call_target="tpu_custom_call" | custom-call | flops 8589934592 | bytes 10485760 | tf_op jit(solution)/shard_map/attention_0/pallas_call | solution.py:180
  36.7 0.0 collective-permute-done.2.refs_1_
  36.7 0.0 copy-start.1
  36.7 0.0 collective-permute-done.3.refs_2_
  36.7 0.0 copy-start.2
  36.7 0.0 collective-permute-done.4.refs_3_
  36.7 0.0 copy-start.3
  36.7 0.7 copy-done.1
  37.4 0.1 copy-done.2
  37.5 0.1 copy-done.3
  37.6 52.7 %attention_1_2_3.1 = (bf16[3072,128]{1,0:T(8,128)(2,1)}, f32[24,128]{1,0:T(8,128)}) custom-call(s32[8,16]{1,0:T(8,128)} %bitcast.22, bf16[1024,128]{1,0:T(8,128)(2,1)} %copy-done.1, bf16[1024,128]{1,0:T(8,128)(2,1)} %copy-done.2, bf16[1024,128]{1,0:T(8,128)(2,1)} %copy-done.3, bf16[8192,128]{1,0:T(8,128)(2,1)} %refs_4_.3, bf16[8192,128]{1,0:T(8,128)(2,1)} %copy-done, ...), custom_call_target="tpu_custom_call" | custom-call | flops 25769803776 | bytes 10485760 | tf_op jit(solution)/shard_map/attention_1_2_3/pallas_call | solution.py:180
  90.3 0.0 all-gather.2.cloned.1.call-done.proj_hbm
  90.3 77.7 %post.1 = bf16[64,2048]{1,0:T(8,128)(2,1)} custom-call(bf16[1,1024,128]{2,1,0:T(8,128)(2,1)} %bitcast.15, bf16[3,1024,128]{2,1,0:T(8,128)(2,1)} %bitcast.14, f32[1,8,128]{2,1,0:T(8,128)} %bitcast.20, f32[3,8,128]{2,1,0:T(8,128)} %bitcast.17, bf16[64,2048]{1,0:T(8,128)(2,1)} %hid_ref.1, s32[6,64]{1,0:T(8,128)} %bitcast.19, f32[1,2048]{1,0:T(1,128)} %bitcast.18, ...), custom_call_target="tpu_custom_call" | custom-call | tf_op jit(solution)/shard_map/post/pallas_call | solution.py:519
  168.1 1.7 copy.14
Async XLA Ops:
  6.5 83.8 %all-gather.2.cloned.1.call-start = ((), (), s32[]{:S(2)}) async-start(), calls=%async_computation | async-start | bytes 8912896 | tf_op jit(solution)/shard_map/all_gather | solution.py:581
  7.3 6.5 %collective-permute-start = (bf16[8192,128]{1,0:T(8,128)(2,1)}, bf16[8192,128]{1,0:T(8,128)(2,1)S(1)}, u32[]{:S(2)}, u32[]{:S(2)}) collective-permute-start(bf16[8192,128]{1,0:T(8,128)(2,1)} %refs_4_.3), channel_id=1, source_target_pairs={{0,16},{16,0},{32,48},{48,32},{64,80},{80,64},{96,112},{112,96},{1... | collective-permute-start | bytes 6291464 | tf_op jit(solution)/shard_map/ppermute | solution.py:584
  7.4 7.5 %collective-permute-start.1 = (bf16[8192,128]{1,0:T(8,128)(2,1)}, bf16[8192,128]{1,0:T(8,128)(2,1)}, u32[]{:S(2)}, u32[]{:S(2)}) collective-permute-start(bf16[8192,128]{1,0:T(8,128)(2,1)} %refs_6_.1), channel_id=1, source_target_pairs={{0,16},{16,0},{32,48},{48,32},{64,80},{80,64},{96,112},{112,96},{1... | collective-permute-start | bytes 6291464 | tf_op jit(solution)/shard_map/ppermute | solution.py:585
  7.8 28.8 %collective-permute-start.2 = (bf16[1024,128]{1,0:T(8,128)(2,1)}, bf16[1024,128]{1,0:T(8,128)(2,1)S(1)}, u32[]{:S(2)}, u32[]{:S(2)}) collective-permute-start(bf16[1024,128]{1,0:T(8,128)(2,1)} %refs_1_.1), channel_id=1, source_target_pairs={{0,96},{16,112},{32,0},{48,16},{64,32},{80,48},{96,64},{112,80},{1... | collective-permute-start | bytes 786440 | tf_op jit(solution)/shard_map/ppermute | solution.py:587
  10.7 26.0 %collective-permute-start.3 = (bf16[1024,128]{1,0:T(8,128)(2,1)}, bf16[1024,128]{1,0:T(8,128)(2,1)S(1)}, u32[]{:S(2)}, u32[]{:S(2)}) collective-permute-start(bf16[1024,128]{1,0:T(8,128)(2,1)} %refs_1_.1), channel_id=1, source_target_pairs={{0,64},{16,80},{32,96},{48,112},{64,0},{80,16},{96,32},{112,48},{1... | collective-permute-start | bytes 786440 | tf_op jit(solution)/shard_map/ppermute | solution.py:587
  11.5 25.2 %collective-permute-start.4 = (bf16[1024,128]{1,0:T(8,128)(2,1)}, bf16[1024,128]{1,0:T(8,128)(2,1)S(1)}, u32[]{:S(2)}, u32[]{:S(2)}) collective-permute-start(bf16[1024,128]{1,0:T(8,128)(2,1)} %refs_1_.1), channel_id=1, source_target_pairs={{0,32},{16,48},{32,64},{48,80},{64,96},{80,112},{96,0},{112,16},{1... | collective-permute-start | bytes 786440 | tf_op jit(solution)/shard_map/ppermute | solution.py:587
  13.8 1.4 copy-start
  36.7 0.7 copy-start.1
  36.7 0.8 copy-start.2
  36.7 0.9 copy-start.3
Sparse Core Ops, SparseCore 0:
  9.5 73.2 all-gather.1
